TPU v7x, 32 devices: a whole 2x2x4 slice. The times are simulated.
32 devices in a mesh: seq: 8 (over z, y), tp: 4 (over x, core).
Axes of the slice: x: 2, y: 2, z: 4, core: 2. Of those that a mesh axis runs over, the one named last changes fastest.
Arguments:
- patches: bfloat16 [8, 256, 1408], P('seq'), may hold values from -6 to 6
- picture_grid: int32 [8, 2], P('seq'), may hold values from 4 to 8, as said below
- vision_qkv: bfloat16 [1408, 3, 1408], P(None, None, 'tp')
- vision_out: bfloat16 [1408, 1408], P('tp'), may hold values from -0.15625 to 0.15625
- merge_weight: bfloat16 [4, 1408, 1408], P('tp'), may hold values from -0.078125 to 0.078125
- picture_block: int32 [8], P('seq'), may hold values from 0 to 7, as said below
- picture_offset: int32 [8], P('seq'), may hold values from 0 to 112, as said below
- tokens: bfloat16 [1024, 1408], P('seq', 'tp'), may hold values from -6 to 6
- prompt_lengths: int32 [16], replicated, may hold values from 1 to 256, 1024 in all
- text_qkv: bfloat16 [1408, 3, 1408], P(None, None, 'tp')
- text_out: bfloat16 [1408, 1408], P('tp'), may hold values from -0.15625 to 0.15625
Outputs:
- hidden_out: bfloat16 [1024, 1408], P('seq')
Inputs may be any that keep to these rules, and one draw needn't show every extreme that they name: `picture_grid`: some picture has both entries equal to 8, another both equal to 4. `picture_block`: the blocks of different pictures differ. picture_offset plus the product of the picture's two picture_grid entries is at most 128. `prompt_lengths`: the lengths sum to 1024.
All inputs are finite; a program needn't handle non-finite values.
Results may differ from a plain program's by a relative error of at most 0.018.
Values may be sent and summed in bfloat16 or wider, within the bound.
A program may use at most 64 MiB of HBM per device.

v0:
```python
import jax
import jax.numpy as jnp
from jax import lax
from jax.sharding import PartitionSpec as P

HEAD = 88
MAXGRID = 16
BLOCK = 128
MERGED = 64


EPSILON = 1e-06
MASKED = -1e30


def passed_along(x, axis, by):
    count = lax.axis_size(axis)
    pairs = [(i, i + by) for i in range(count) if 0 <= i + by < count]
    return lax.ppermute(x, axis, pairs)


def normalize(values):
    values = values.astype(jnp.float32)
    centre = jnp.mean(values, axis=-1, keepdims=True)
    shifted = values - centre
    spread = jnp.mean(shifted * shifted, axis=-1, keepdims=True)
    return (shifted * lax.rsqrt(spread + EPSILON)).astype(jnp.bfloat16)


def merge_cells(normed):
    halves = MAXGRID // 2
    shaped = normed.reshape(halves, 2, halves, 2, normed.shape[-1])
    return shaped.transpose(0, 2, 1, 3, 4).reshape(halves * halves, 4, normed.shape[-1])


def merged_positions(half_grid, block_index, offset):
    halves = MAXGRID // 2
    cells = jnp.arange(MERGED, dtype=jnp.int32)
    row_cell = cells // halves
    col_cell = cells % halves
    usable = (row_cell < half_grid[0]) & (col_cell < half_grid[1])
    target = block_index * BLOCK + offset + row_cell * half_grid[1] + col_cell
    return jnp.where(usable, target, -1)


def prompt_starts(prompt_lengths, positions):
    ends = jnp.cumsum(prompt_lengths)
    picked = jnp.where(ends[None, :] <= positions[:, None], prompt_lengths[None, :], 0)
    return jnp.sum(picked, axis=1)


def pick_pictures(rows_all, slots_all, tok_rows):
    first_slot = slots_all[:, 0]
    sources = jnp.arange(slots_all.shape[0], dtype=jnp.int32)
    hit = (first_slot >= 0) & (first_slot < tok_rows) & (first_slot // BLOCK == 0)
    which = jnp.sum(jnp.where(hit, sources, 0))
    present = jnp.any(hit)
    picked_rows = lax.dynamic_index_in_dim(rows_all, which, 0, keepdims=False)
    slot_row = lax.dynamic_index_in_dim(slots_all, which, 0, keepdims=False)
    picked_slots = jnp.where(present, slot_row, -1).astype(jnp.int32)
    return (picked_rows, picked_slots)


def mix_heads(partial_value):
    return lax.psum(partial_value.astype(jnp.bfloat16), "tp").astype(jnp.float32)


def local(
    patches,
    picture_grid,
    vision_qkv,
    vision_out,
    merge_weight,
    picture_block,
    picture_offset,
    tokens,
    prompt_lengths,
    text_qkv,
    text_out,
):
    scale = HEAD ** (-0.5)
    model_width = patches.shape[2]
    local_width = vision_qkv.shape[2]
    local_heads = local_width // HEAD
    picture = patches[0]
    half_grid = picture_grid[0]
    patch_count = picture.shape[0]
    normed = normalize(picture)
    projected = jnp.dot(
        normed, vision_qkv.reshape(model_width, 3 * local_width), preferred_element_type=jnp.float32
    )
    projected = projected.astype(jnp.bfloat16).reshape(patch_count, 3, local_heads, HEAD)
    scores = (
        jnp.einsum(
            "qhe,khe->hqk", projected[:, 0], projected[:, 1], preferred_element_type=jnp.float32
        )
        * scale
    )
    cells = jnp.arange(patch_count, dtype=jnp.int32)
    usable = (cells // MAXGRID < 2 * half_grid[0]) & (cells % MAXGRID < 2 * half_grid[1])
    allowed = usable[None, None, :]
    scores = jnp.where(allowed, scores, MASKED)
    row_max = jnp.max(scores, axis=-1, keepdims=True)
    expons = jnp.where(allowed, jnp.exp(scores - row_max), 0.0)
    row_total = jnp.sum(expons, axis=-1)
    weights = expons.astype(jnp.bfloat16)
    summed = jnp.einsum(
        "hqk,khe->qhe", weights, projected[:, 2], preferred_element_type=jnp.float32
    )
    context = (
        (summed / jnp.transpose(row_total)[:, :, None])
        .astype(jnp.bfloat16)
        .reshape(patch_count, local_width)
    )
    hidden = picture.astype(jnp.float32) + mix_heads(
        jnp.dot(context, vision_out, preferred_element_type=jnp.float32)
    )
    merged_in = merge_cells(normalize(hidden))
    parts_here = merge_weight.shape[0]
    chosen = lax.dynamic_slice_in_dim(merged_in, lax.axis_index("tp") * parts_here, parts_here, 1)
    term = jnp.einsum("mkd,kde->me", chosen, merge_weight, preferred_element_type=jnp.float32)
    share = lax.psum_scatter(term.astype(jnp.bfloat16), "tp", scatter_dimension=1, tiled=True)
    tok_rows = tokens.shape[0]
    seq_count = lax.axis_size("seq")
    own_start = lax.axis_index("seq") * tok_rows
    target = merged_positions(half_grid, picture_block[0], picture_offset[0])
    owner = jnp.where(target >= 0, target // tok_rows, -1)
    local_target = jnp.where(target >= 0, target % tok_rows, -1)
    routed = jnp.arange(seq_count, dtype=jnp.int32)[:, None] == owner[None, :]
    send_rows = jnp.where(routed[:, :, None], share[None], jnp.zeros((), jnp.bfloat16))
    send_slots = jnp.where(routed, local_target[None, :], -1)
    got_rows, got_slots = (
        lax.all_to_all(send_rows, "seq", split_axis=0, concat_axis=0, tiled=True),
        lax.all_to_all(send_slots, "seq", split_axis=0, concat_axis=0, tiled=True),
    )
    arrived, slots = pick_pictures(got_rows, got_slots, tok_rows)
    table = (jnp.arange(tok_rows, dtype=jnp.int32)[:, None] == slots[None, :]).astype(jnp.bfloat16)
    placed = jnp.dot(table, arrived, preferred_element_type=jnp.float32).astype(jnp.bfloat16)
    covered = jnp.max(table, axis=1) > 0
    prompt_share = jnp.where(covered[:, None], placed, tokens)
    prompt_in = lax.all_gather(prompt_share, "tp", axis=1, tiled=True)
    normed = normalize(prompt_in)
    projected = jnp.dot(
        normed, text_qkv.reshape(model_width, 3 * local_width), preferred_element_type=jnp.float32
    )
    projected = projected.astype(jnp.bfloat16).reshape(tok_rows, 3, local_width)
    query_rows = projected[:, 0].reshape(tok_rows, local_heads, HEAD)
    key_values = projected[:, 1:]
    query_pos = own_start + jnp.arange(tok_rows, dtype=jnp.int32)
    query_start = prompt_starts(prompt_lengths, query_pos)

    def attend(carry, pair, key_first):
        old_max, old_total, old_summed = carry
        count = pair.shape[0]
        key_rows = pair[:, 0].reshape(count, local_heads, HEAD)
        value_rows = pair[:, 1].reshape(count, local_heads, HEAD)
        block_scores = (
            jnp.einsum("qhe,khe->hqk", query_rows, key_rows, preferred_element_type=jnp.float32)
            * scale
        )
        key_pos = key_first + jnp.arange(count, dtype=jnp.int32)
        visible = (
            (key_pos[None, :] <= query_pos[:, None]) & (key_pos[None, :] >= query_start[:, None])
        )[None]
        block_scores = jnp.where(visible, block_scores, MASKED)
        new_max = jnp.maximum(old_max, jnp.max(block_scores, axis=-1))
        block_exp = jnp.where(visible, jnp.exp(block_scores - new_max[..., None]), 0.0)
        factor = jnp.exp(old_max - new_max)
        new_total = old_total * factor + jnp.sum(block_exp, axis=-1)
        gained = jnp.einsum(
            "hqk,khe->hqe",
            block_exp.astype(jnp.bfloat16),
            value_rows,
            preferred_element_type=jnp.float32,
        )
        return (new_max, new_total, old_summed * factor[..., None] + gained)

    def visit(carry, pair, key_first):
        return attend(carry, pair, key_first)

    def fold_piece(carry, piece, start):
        count = piece.shape[0]
        block_rows = count
        block_count = count // block_rows
        grouped = piece.reshape(block_count, block_rows, 2, local_width)

        def inner(state, item):
            rows_here, index = item
            return (visit(state, rows_here, start + index * block_rows), None)

        return lax.scan(inner, carry, (grouped, jnp.arange(block_count, dtype=jnp.int32)))[0]

    initial = (
        jnp.full((local_heads, tok_rows), MASKED, jnp.float32),
        jnp.zeros((local_heads, tok_rows), jnp.float32),
        jnp.zeros((local_heads, tok_rows, HEAD), jnp.float32),
    )
    hop_count = (seq_count + 3) // 4
    own_fold = fold_piece(initial, key_values, own_start)

    def hop(step, state):
        gathered, moving = state
        moving = passed_along(moving, "seq", 1)
        gathered = fold_piece(gathered, moving, own_start - (step + 1) * tok_rows)
        return (gathered, moving)

    final_max, final_total, final_summed = lax.fori_loop(0, hop_count, hop, (own_fold, key_values))[
        0
    ]
    context = (
        (final_summed / final_total[..., None])
        .transpose(1, 0, 2)
        .reshape(tok_rows, local_width)
        .astype(jnp.bfloat16)
    )
    output = prompt_in.astype(jnp.float32) + mix_heads(
        jnp.dot(context, text_out, preferred_element_type=jnp.float32)
    )
    return output.astype(jnp.bfloat16)


def solution(mesh):
    placed = (
        P("seq", None, None),
        P("seq", None),
        P(None, None, "tp"),
        P("tp", None),
        P("tp", None, None),
        P("seq"),
        P("seq"),
        P("seq", "tp"),
        P(),
        P(None, None, "tp"),
        P("tp", None),
    )
    return jax.shard_map(
        local, mesh=mesh, in_specs=placed, out_specs=P("seq", None), check_vma=False
    )
```

profile of v0, /device:TPU:0, one launch (start us, length us, event | category | flops | bytes accessed | tf_op | source)
XLA Modules:
  0.0 183.3 jit_solution(8315678257147830652)
XLA Ops:
  6.5 1.5 fusion.73
  9.3 1.4 convert_reduce_fusion
  10.7 1.4 fusion.20
  12.1 1.1 convolution_convert_fusion.1
  13.3 1.3 fusion.25
  14.6 0.6 fusion.74
  15.2 2.6 %fusion.29 = bf16[256,4,88]{0,2,1:T(8,128)(2,1)} fusion(bf16[256,3,4,88]{0,3,2,1:T(8,128)(2,1)S(1)} %bitcast.118, f32[256,4]{0,1:T(4,128)S(1)} %bitcast.124, f32[4,256,256]{1,2,0:T(8,128)} %fusion.25, pred[256]{0:T(512)(128)(4,1)S(1)} %compare_and_fusion.2), kind=kOutput, calls=%fused_computation.44 | convolution fusion | flops 47105280 | bytes 2462208 | tf_op jit(solution)/shard_map/hqk,khe->qhe/dot_general | solution.py:107
  17.8 2.8 %convolution_convert_fusion = bf16[256,1408]{1,0:T(8,128)(2,1)} fusion(bf16[256,352]{0,1:T(8,128)(2,1)} %bitcast.119, bf16[352,1408]{1,0:T(8,128)(2,1)} %param.16), kind=kOutput, calls=%fused_computation.19 | convolution fusion | flops 254115840 | bytes 1892352 | tf_op jit(solution)/shard_map/dot_general | solution.py:116
  21.9 1.3 compare_select_fusion.8
  23.2 1.3 compare_select_fusion.7
  24.5 0.6 compare_select_fusion
  25.1 7.3 %all-to-all-start = ((s32[8,1,64]{2,1,0:T(1,128)}), s32[8,1,64]{2,1,0:T(1,128)S(1)}, u32[]{:S(2)}, u32[]{:S(2)}) async-start(s32[8,1,64]{2,1,0:T(1,128)} %compare_select_fusion), calls=%async_computation | async-start | bytes 8192 | tf_op jit(solution)/shard_map/all_to_all | solution.py:134
  32.7 24.9 %all-reduce.3.cloned.1.call-done = bf16[256,1408]{1,0:T(8,128)(2,1)} async-done(((bf16[256,1408]{1,0:T(8,128)(2,1)}), bf16[256,1408]{1,0:T(8,128)(2,1)}) %all-reduce.3.cloned.1.call-update) | async-done | bytes 720912 | tf_op jit(solution)/shard_map/psum | solution.py:65
  57.7 1.7 fusion.27
  59.4 0.4 multiply_reduce_fusion
  59.8 1.1 multiply_convert_fusion
  60.9 2.7 %reshape.423 = bf16[8,2,8,2,1408]{4,3,2,1,0:T(2,128)(2,1)} reshape(bf16[256,1408]{1,0:T(8,128)(2,1)} %multiply_convert_fusion) | data formatting | bytes 1441792 | tf_op jit(solution)/shard_map/reshape | solution.py:32
  63.7 1.2 copy.34
  64.9 2.9 %fusion.13 = bf16[64,1408]{1,0:T(8,128)(2,1)S(1)} fusion(bf16[1,1408,1408]{2,1,0:T(8,128)(2,1)} %param.17, bf16[64,4,1408]{2,0,1:T(8,128)(2,1)S(1)} %bitcast.110, s32[]{:T(128)S(6)} %select_n.201), kind=kOutput, calls=%fused_computation.23 | convolution fusion | flops 253845504 | bytes 4325380 | tf_op jit(solution)/shard_map/mkd,kde->me/dot_general | solution.py:121
  67.7 0.9 copy.43
  68.9 20.6 %reduce-scatter.4.cloned.1.call-done = bf16[352,64]{1,0:T(8,128)(2,1)} async-done(((bf16[1408,64]{1,0:T(8,128)(2,1)}), bf16[352,64]{1,0:T(8,128)(2,1)}) %reduce-scatter.4.cloned.1.call-update) | async-done | bytes 45072
  89.5 1.0 copy.44
  90.4 0.9 broadcast_select_fusion
  91.3 5.5 %all-to-all-start.1 = ((bf16[8,64,352]{2,1,0:T(8,128)(2,1)}), bf16[8,64,352]{2,1,0:T(8,128)(2,1)S(1)}, u32[]{:S(2)}, u32[]{:S(2)}) async-start(bf16[8,64,352]{2,1,0:T(8,128)(2,1)} %broadcast_select_fusion), calls=%async_computation.1 | async-start | bytes 786432 | tf_op jit(solution)/shard_map/all_to_all | solution.py:133
  96.9 0.6 fusion.69
  97.5 0.7 select_reduce_fusion.1
  100.1 0.7 fusion.62
  100.9 7.7 %all-to-all-done.1 = bf16[8,64,352]{2,1,0:T(8,128)(2,1)S(1)} async-done(((bf16[8,64,352]{2,1,0:T(8,128)(2,1)}), bf16[8,64,352]{2,1,0:T(8,128)(2,1)S(1)}, u32[]{:S(2)}, u32[]{:S(2)}) %all-to-all-start.1) | async-done | bytes 360480 | tf_op jit(solution)/shard_map/all_to_all | solution.py:133
  108.5 0.2 fusion.31
  108.8 6.1 %all_gather.3 = bf16[128,1408]{0,1:T(8,128)(2,1)S(1)} all-gather(bf16[128,352]{0,1:T(8,128)(2,1)S(1)} %fusion.31), channel_id=1, replica_groups=mesh['seq'=8,'tp'=4] {'tp'}, dimensions={1}, use_global_device_ids=true | all-gather | bytes 450560 | tf_op jit(solution)/shard_map/all_gather | solution.py:141
  115.3 2.8 %convolution_convert_fusion.2 = bf16[128,1056]{0,1:T(8,128)(2,1)S(1)} fusion(bf16[1408,1056]{0,1:T(8,128)(2,1)} %bitcast.123, bf16[128,1408]{0,1:T(8,128)(2,1)S(1)} %all_gather.3, f32[128]{0:T(128)S(1)} %add_rsqrt_fusion.2, f32[128]{0:T(128)S(1)} %broadcast_multiply_fusion.2), kind=kOutput, calls=%fused_computation.21 | convolution fusion | flops 381489152 | bytes 3605504 | tf_op jit(solution)/shard_map/dot_general | solution.py:143
  118.1 0.7 slice.83
  118.8 0.3 fusion.75
  119.3 18.7 %while.43 = (s32[]{:T(128)}, f32[4,128]{1,0:T(4,128)S(1)}, f32[4,128]{1,0:T(4,128)S(1)}, f32[4,128,88]{1,2,0:T(8,128)S(1)}, bf16[128,2,352]{0,2,1:T(8,128)(2,1)}...) while((s32[]{:T(128)}, f32[4,128]{1,0:T(4,128)S(1)}, ...), condition=%wide.region_20.21_spmd.clone.clone, body=%wide.region_17.20_spmd.clone.clone.sunk | while | flops 23799044 | bytes 2960045 | solution.py:207
  119.4 3.4 %collective-permute-start = (bf16[128,2,352]{0,2,1:T(8,128)(2,1)}, bf16[128,2,352]{0,2,1:T(8,128)(2,1)S(1)}, u32[]{:S(2)}, u32[]{:S(2)}) collective-permute-start(bf16[128,2,352]{0,2,1:T(8,128)(2,1)} %get-tuple-element.455), channel_id=1, source_target_pairs={{0,4},{4,8},{8,12},{12,16},{16,20},{20,24},{24,28},{1,5},{5,9},{9,... | collective-permute-start | bytes 540680 | tf_op jit(solution)/shard_map/while/body/eval_jaxpr/ppermute | solution.py:19
  122.8 4.5 %collective-permute-done = bf16[128,2,352]{0,2,1:T(8,128)(2,1)S(1)} collective-permute-done((bf16[128,2,352]{0,2,1:T(8,128)(2,1)}, bf16[128,2,352]{0,2,1:T(8,128)(2,1)S(1)}, u32[]{:S(2)}, u32[]{:S(2)}) %collective-permute-start) | collective-permute-done | bytes 180256 | tf_op jit(solution)/shard_map/while/body/eval_jaxpr/ppermute | solution.py:19
  127.3 0.3 fusion.101
  127.7 0.2 convolution_add_fusion.3
  128.0 0.7 copy.60
  128.6 4.3 %collective-permute-start = (bf16[128,2,352]{0,2,1:T(8,128)(2,1)}, bf16[128,2,352]{0,2,1:T(8,128)(2,1)S(1)}, u32[]{:S(2)}, u32[]{:S(2)}) collective-permute-start(bf16[128,2,352]{0,2,1:T(8,128)(2,1)} %get-tuple-element.455), channel_id=1, source_target_pairs={{0,4},{4,8},{8,12},{12,16},{16,20},{20,24},{24,28},{1,5},{5,9},{9,... | collective-permute-start | bytes 540680 | tf_op jit(solution)/shard_map/while/body/eval_jaxpr/ppermute | solution.py:19
  133.0 3.7 %collective-permute-done = bf16[128,2,352]{0,2,1:T(8,128)(2,1)S(1)} collective-permute-done((bf16[128,2,352]{0,2,1:T(8,128)(2,1)}, bf16[128,2,352]{0,2,1:T(8,128)(2,1)S(1)}, u32[]{:S(2)}, u32[]{:S(2)}) %collective-permute-start) | collective-permute-done | bytes 180256 | tf_op jit(solution)/shard_map/while/body/eval_jaxpr/ppermute | solution.py:19
  136.7 0.3 fusion.101
  137.1 0.2 convolution_add_fusion.3
  137.3 0.7 copy.60
  138.0 2.5 %convolution_convert_fusion.3 = bf16[128,1408]{0,1:T(8,128)(2,1)} fusion(bf16[128,352]{0,1:T(8,128)(2,1)S(1)} %bitcast.114, bf16[352,1408]{1,0:T(8,128)(2,1)} %param.23), kind=kOutput, calls=%fused_computation.22 | convolution fusion | flops 127057920 | bytes 1441792 | tf_op jit(solution)/shard_map/dot_general | solution.py:217
  140.6 32.5 %all-reduce.5.cloned.1.call-done = bf16[128,1408]{0,1:T(8,128)(2,1)} async-done(((bf16[128,1408]{0,1:T(8,128)(2,1)}), bf16[128,1408]{0,1:T(8,128)(2,1)}) %all-reduce.5.cloned.1.call-update) | async-done | bytes 360464 | tf_op jit(solution)/shard_map/psum | solution.py:65
  173.1 1.8 fusion.36
  174.9 1.9 %copy.38 = bf16[128,1408]{1,0:T(8,128)(2,1)} copy(bf16[128,1408]{0,1:T(8,128)(2,1)} %fusion.36) | data formatting | bytes 720896 | tf_op jit(solution)/shard_map/convert_element_type | solution.py:219
  (62 shorter events, 2.0 us)
Async XLA Ops:
  6.5 5.6 %copy-start = (bf16[1408,3,352]{0,2,1:T(8,128)(2,1)S(1)}, bf16[1408,3,352]{0,2,1:T(8,128)(2,1)}, u32[]{:S(2)}) copy-start(bf16[1408,3,352]{0,2,1:T(8,128)(2,1)} %param.15) | copy-start | bytes 8921092
  6.5 51.1 %all-reduce.3.cloned.1.call-start = ((), (), s32[]{:S(2)}) async-start(), calls=%async_computation.3 | async-start | bytes 1441792 | tf_op jit(solution)/shard_map/psum | solution.py:65
  9.3 2.9 %copy-start.1 = (bf16[1,256,1408]{2,1,0:T(8,128)(2,1)S(1)}, bf16[1,256,1408]{2,1,0:T(8,128)(2,1)}, u32[]{:S(2)}) copy-start(bf16[1,256,1408]{2,1,0:T(8,128)(2,1)} %param.13) | copy-start | bytes 2162692
  17.8 14.6 %copy-start.7 = (s32[16]{0:T(128)S(1)}, s32[16]{0:T(128)}, u32[]{:S(2)}) copy-start(s32[16]{0:T(128)} %param.21) | copy-start | bytes 196
  25.1 43.7 %all-to-all-start = ((s32[8,1,64]{2,1,0:T(1,128)}), s32[8,1,64]{2,1,0:T(1,128)S(1)}, u32[]{:S(2)}, u32[]{:S(2)}) async-start(s32[8,1,64]{2,1,0:T(1,128)} %compare_select_fusion), calls=%async_computation | async-start | bytes 8192 | tf_op jit(solution)/shard_map/all_to_all | solution.py:134
  32.3 57.1 %reduce-scatter.4.cloned.1.call-start = ((), (), s32[]{:S(2)}) async-start(), calls=%async_computation.5 | async-start | bytes 450560
  57.7 1.7 copy-start.2
  57.7 1.8 copy-start.3
  67.7 40.8 %copy-start.6 = (bf16[128,352]{0,1:T(8,128)(2,1)S(1)}, bf16[128,352]{0,1:T(8,128)(2,1)}, u32[]{:S(2)}) copy-start(bf16[128,352]{0,1:T(8,128)(2,1)} %param.20) | copy-start | bytes 270340
  91.3 17.2 %all-to-all-start.1 = ((bf16[8,64,352]{2,1,0:T(8,128)(2,1)}), bf16[8,64,352]{2,1,0:T(8,128)(2,1)S(1)}, u32[]{:S(2)}, u32[]{:S(2)}) async-start(bf16[8,64,352]{2,1,0:T(8,128)(2,1)} %broadcast_select_fusion), calls=%async_computation.1 | async-start | bytes 786432 | tf_op jit(solution)/shard_map/all_to_all | solution.py:133
  96.8 76.2 %all-reduce.5.cloned.1.call-start = ((), (), s32[]{:S(2)}) async-start(), calls=%async_computation.4 | async-start | bytes 720896 | tf_op jit(solution)/shard_map/psum | solution.py:65
  114.8 3.2 %copy-start.4 = (bf16[128,1408]{0,1:T(8,128)(2,1)}, bf16[128,1408]{0,1:T(8,128)(2,1)S(1)}, u32[]{:S(2)}) copy-start(bf16[128,1408]{0,1:T(8,128)(2,1)S(1)} %all_gather.3) | copy-start | bytes 1081348
  119.4 8.0 %collective-permute-start = (bf16[128,2,352]{0,2,1:T(8,128)(2,1)}, bf16[128,2,352]{0,2,1:T(8,128)(2,1)S(1)}, u32[]{:S(2)}, u32[]{:S(2)}) collective-permute-start(bf16[128,2,352]{0,2,1:T(8,128)(2,1)} %get-tuple-element.455), channel_id=1, source_target_pairs={{0,4},{4,8},{8,12},{12,16},{16,20},{20,24},{24,28},{1,5},{5,9},{9,... | collective-permute-start | bytes 540680 | tf_op jit(solution)/shard_map/while/body/eval_jaxpr/ppermute | solution.py:19
  128.6 8.1 %collective-permute-start = (bf16[128,2,352]{0,2,1:T(8,128)(2,1)}, bf16[128,2,352]{0,2,1:T(8,128)(2,1)S(1)}, u32[]{:S(2)}, u32[]{:S(2)}) collective-permute-start(bf16[128,2,352]{0,2,1:T(8,128)(2,1)} %get-tuple-element.455), channel_id=1, source_target_pairs={{0,4},{4,8},{8,12},{12,16},{16,20},{20,24},{24,28},{1,5},{5,9},{9,... | collective-permute-start | bytes 540680 | tf_op jit(solution)/shard_map/while/body/eval_jaxpr/ppermute | solution.py:19
  138.0 35.1 %copy-start.5 = (bf16[128,1408]{0,1:T(8,128)(2,1)S(1)}, bf16[128,1408]{0,1:T(8,128)(2,1)}, u32[]{:S(2)}) copy-start(bf16[128,1408]{0,1:T(8,128)(2,1)} %copy-done.4) | copy-start | bytes 1081348
Sparse Core Ops, SparseCore 0:
  20.7 36.8 all-reduce.2
  68.8 20.6 reduce-scatter.3
  140.7 32.3 all-reduce.4
where the time goes:
time: 184 us; the launch traced here: 183 us
  waiting for transfers between devices  93.8 us (51%)
  starting transfers between devices  20.5 us (11%)
  matrix products  18.3 us (10%)
  between operations  17.7 us (10%)
  other arithmetic  15.3 us (8%)
  local copies, waits for them, and re-layouts  11.5 us (6%)
  blocking collectives  6.06 us (3%)
    psum x2, waiting for transfers between devices, mix_heads(): lax.psum(partial_value.astype(jnp.bfloat16), 'tp').astype(jnp.float32)  57.4 us
    unnamed x4, waiting for transfers between devices  20.6 us
    ppermute x2, waiting for transfers between devices, passed_along(): return lax.ppermute(x, axis, pairs)  8.17 us
    all_to_all x1, waiting for transfers between devices, local(): lax.all_to_all(send_rows, 'seq', split_axis=0, concat_axis=0, tiled=True)  7.65 us
    ppermute x2, starting transfers between devices, passed_along(): return lax.ppermute(x, axis, pairs)  7.63 us
    all_to_all x1, starting transfers between devices, local(): lax.all_to_all(send_slots, 'seq', split_axis=0, concat_axis=0, tiled=True)  7.28 us
    all_gather x1, blocking collectives, local(): prompt_in = lax.all_gather(prompt_share, 'tp', axis=1, tiled=True)  6.06 us
    all_to_all x1, starting transfers between devices, local(): lax.all_to_all(send_rows, 'seq', split_axis=0, concat_axis=0, tiled=True)  5.52 us
  transfers between devices with their start and end apart: 7, of which 6 were waited for; matrix products, arithmetic and copies ran while one was open for 9% of the time, Pallas kernels for 0%

commit v1 on v0

v1 whole, which is shorter than its diff:
```python
import functools

import jax
import jax.numpy as jnp
from jax import lax
from jax.experimental import pallas as pl
from jax.experimental.pallas import tpu as pltpu
from jax.sharding import PartitionSpec as P

HEAD = 88
MAXGRID = 16
MERGED = 64
EPSILON = 1e-06
MASKED = -1e30
F32 = jnp.float32
BF16 = jnp.bfloat16


def normalize(values):
    values = values.astype(F32)
    centre = jnp.mean(values, axis=-1, keepdims=True)
    shifted = values - centre
    spread = jnp.mean(shifted * shifted, axis=-1, keepdims=True)
    return (shifted * lax.rsqrt(spread + EPSILON)).astype(BF16)


def matmul(a, b):
    return jnp.dot(a, b, preferred_element_type=F32)


def matmul_rows(a, b):
    return lax.dot_general(a, b, (((1,), (1,)), ((), ())), preferred_element_type=F32)


def attention(query, keys, values, allowed):
    width = query.shape[1]
    parts = [None] * (-(-width // 128))
    for head in range(width // HEAD):
        first, last = head * HEAD, (head + 1) * HEAD
        low, high = first // 128 * 128, min(width, -(-last // 128) * 128)
        lane = lax.broadcasted_iota(jnp.int32, (1, high - low), 1) + low
        inside = (lane >= first) & (lane < last)
        own_query = jnp.where(inside, query[:, low:high].astype(F32), 0.0).astype(BF16)
        own_values = jnp.where(inside, values[:, low:high].astype(F32), 0.0).astype(BF16)
        scores = matmul_rows(own_query, keys[:, low:high])
        scores = jnp.where(allowed, scores * HEAD ** (-0.5), MASKED)
        expons = jnp.exp(scores - jnp.max(scores, axis=-1, keepdims=True))
        total = jnp.sum(expons, axis=-1, keepdims=True)
        context = matmul(expons.astype(BF16), own_values) / total
        for at in range(low, high, 128):
            piece = context[:, at - low : min(high, at + 128) - low]
            slot = at // 128
            parts[slot] = piece if parts[slot] is None else parts[slot] + piece
    return [part.astype(BF16) for part in parts]


def kernel(
    seq_count,
    hops,
    patches,
    grid,
    vqkv,
    vout,
    merge,
    block,
    offset,
    tokens,
    lengths,
    tqkv,
    tout,
    out,
    patch_v,
    vqkv_v,
    vout_v,
    merge_v,
    tqkv_v,
    tout_v,
    tok_v,
    meta_v,
    context_v,
    half_send,
    half_got,
    cross_send,
    cross_got,
    term_v,
    term_got,
    gathered,
    chosen_v,
    key_v,
    value_v,
    text_context,
    last_send,
    last_got,
    load_sem,
    tok_s,
    tok_r,
    meta_s,
    meta_r,
    half_s,
    half_r,
    cross_s,
    cross_r,
    term_s,
    term_r,
    gather_s,
    gather_r,
    chosen_s,
    chosen_r,
    key_s,
    key_r,
    value_s,
    value_r,
    last_s,
    last_r,
    out_s,
    out_r,
):
    me = lax.axis_index("seq")
    t = lax.axis_index("tp")
    tp = 4
    rows = tokens.shape[0]
    width = tokens.shape[1]
    sibling = t + 1 - 2 * lax.rem(t, 2)
    across = lax.rem(t + 2, 4)
    opposite = 3 - t

    def load(source, target, index):
        copy = pltpu.make_async_copy(source, target, load_sem.at[index])
        copy.start()
        return copy

    def to_tp(source, target, send, recv, peer):
        return pltpu.make_async_remote_copy(
            src_ref=source,
            dst_ref=target,
            send_sem=send,
            recv_sem=recv,
            device_id=(me, peer),
            device_id_type=pl.DeviceIdType.MESH,
        )

    def to_seq(source, target, send, recv, peer):
        return pltpu.make_async_remote_copy(
            src_ref=source,
            dst_ref=target,
            send_sem=send,
            recv_sem=recv,
            device_id=(peer, t),
            device_id_type=pl.DeviceIdType.MESH,
        )

    load_patches = load(patches.at[0], patch_v, 0)
    load_vqkv = load(vqkv, vqkv_v, 1)
    load_vout = load(vout, vout_v, 2)
    load_merge = load(merge.at[0], merge_v, 3)
    load_tqkv = load(tqkv, tqkv_v, 4)
    load_tout = load(tout, tout_v, 5)

    barrier = pltpu.get_barrier_semaphore()
    for d in range(1, tp):
        pl.semaphore_signal(
            barrier, inc=1, device_id=(me, lax.rem(t + d, tp)), device_id_type=pl.DeviceIdType.MESH
        )

    def greet(d, _):
        pl.semaphore_signal(
            barrier,
            inc=1,
            device_id=(lax.rem(me + d, seq_count), t),
            device_id_type=pl.DeviceIdType.MESH,
        )
        return 0

    lax.fori_loop(1, seq_count, greet, 0)

    half_rows, half_cols = grid[0, 0], grid[0, 1]
    count = patch_v.shape[0]
    slot = lax.broadcasted_iota(jnp.int32, (count, count), 0)
    cell = slot % MERGED
    part = slot // MERGED
    source = (2 * (cell // 8) + part // 2) * MAXGRID + 2 * (cell % 8) + part % 2
    order = (source == lax.broadcasted_iota(jnp.int32, (count, count), 1)).astype(F32).astype(BF16)
    load_patches.wait()
    picture = matmul(order, patch_v[...]).astype(BF16)
    patch_v[...] = picture
    normed = normalize(picture)
    key_slot = lax.broadcasted_iota(jnp.int32, (1, count), 1)
    key_cell = key_slot % MERGED
    key_allowed = (key_cell // 8 < half_rows) & (key_cell % 8 < half_cols)
    load_vqkv.wait()
    query = matmul_rows(normed, vqkv_v[0]).astype(BF16)
    keys = matmul_rows(normed, vqkv_v[1]).astype(BF16)
    values = matmul_rows(normed, vqkv_v[2]).astype(BF16)
    for index, piece in enumerate(attention(query, keys, values, key_allowed)):
        context_v[:, index * 128 : index * 128 + piece.shape[1]] = piece

    field = lax.broadcasted_iota(jnp.int32, (8, 128), 0)
    meta_v[me] = jnp.where(
        field == 0,
        half_rows,
        jnp.where(field == 1, half_cols, jnp.where(field == 2, block[0], offset[0])),
    )
    tok_v[t] = tokens[...]
    pl.semaphore_wait(barrier, tp - 1 + seq_count - 1)

    load_vout.wait()

    def partial_rows(which):
        start = pl.multiple_of(which * MERGED, MERGED)
        return matmul(context_v[pl.ds(start, MERGED), :], vout_v[...])

    half_copies = []
    for index, which in ((1, opposite), (0, sibling)):
        half_send[index] = partial_rows(which).astype(BF16)
        copy = to_tp(
            half_send.at[index], half_got.at[index], half_s.at[index], half_r.at[index], sibling
        )
        copy.start()
        half_copies.append(copy)
    far = partial_rows(across)
    half_copies[0].wait_recv()
    cross_send[...] = (far + half_got[1].astype(F32)).astype(BF16)
    cross = to_tp(cross_send, cross_got, cross_s.at[0], cross_r.at[0], across)
    cross.start()
    near = partial_rows(t)
    half_copies[1].wait_recv()
    own_start = pl.multiple_of(t * MERGED, MERGED)
    hidden = (
        patch_v[pl.ds(own_start, MERGED), :].astype(F32) + near + half_got[0].astype(F32)
    )

    tok_copies = []
    for d in range(1, tp):
        copy = to_tp(tokens, tok_v.at[t], tok_s.at[d], tok_r.at[d], lax.rem(t + d, tp))
        copy.start()
        tok_copies.append(copy)

    def send_meta(d, _):
        to_seq(
            meta_v.at[me], meta_v.at[me], meta_s.at[d], meta_r.at[d], lax.rem(me + d, seq_count)
        ).start()
        return 0

    lax.fori_loop(1, seq_count, send_meta, 0)

    load_merge.wait()
    cross.wait_recv()
    merged_in = normalize(hidden + cross_got[...].astype(F32))

    share = MERGED // tp
    term_v[...] = matmul(merged_in, merge_v[...])
    term_copies = []
    for d in range(1, tp):
        peer = lax.rem(t + d, tp)
        last_send[d, 0:share, :] = term_v[
            pl.ds(pl.multiple_of(peer * share, share), share), :
        ].astype(BF16)
        copy = to_tp(
            last_send.at[d, pl.ds(0, share), :],
            term_got.at[d],
            term_s.at[d],
            term_r.at[d],
            peer,
        )
        copy.start()
        term_copies.append(copy)
    merged = term_v[pl.ds(pl.multiple_of(t * share, share), share), :]
    for d, copy in enumerate(term_copies, 1):
        copy.wait_recv()
        merged = merged + term_got[d].astype(F32)
    gathered[me] = merged.astype(BF16)

    def send_merged(d, _):
        to_seq(
            gathered.at[me],
            gathered.at[me],
            gather_s.at[d],
            gather_r.at[d],
            lax.rem(me + d, seq_count),
        ).start()
        return 0

    lax.fori_loop(1, seq_count, send_merged, 0)

    for copy in tok_copies:
        copy.wait_recv()
    token_rows = jnp.concatenate([tok_v[i].astype(F32) for i in range(tp)], axis=1)
    position = lax.broadcasted_iota(jnp.int32, (rows, 1), 0) + me * rows
    start = jnp.zeros((rows, 1), jnp.int32)
    end = jnp.int32(0)
    for index in range(lengths.shape[0]):
        end = end + lengths[index]
        start = jnp.where(end <= position, end, start)

    def meta_arrived(d, _):
        to_seq(
            meta_v.at[me], meta_v.at[me], meta_s.at[d], meta_r.at[d], lax.rem(me + d, seq_count)
        ).wait()
        return 0

    lax.fori_loop(1, seq_count, meta_arrived, 0)

    def merged_arrived(d, _):
        to_seq(
            gathered.at[me],
            gathered.at[me],
            gather_s.at[d],
            gather_r.at[d],
            lax.rem(me + d, seq_count),
        ).wait()
        return 0

    lax.fori_loop(1, seq_count, merged_arrived, 0)

    def choose(index, state):
        cells_sum, meta_sum, present = state
        about = meta_v[index]
        hit = (about[2:3, :] == me).astype(jnp.int32)
        rows_here = gathered[index].astype(F32) * hit[:, 0:1].astype(F32)
        return cells_sum + rows_here, meta_sum + about * hit, present + hit

    cells_sum, about, present = lax.fori_loop(
        0,
        seq_count,
        choose,
        (
            jnp.zeros((share, tout.shape[1]), F32),
            jnp.zeros((8, 128), jnp.int32),
            jnp.zeros((1, 128), jnp.int32),
        ),
    )
    own_cells = pl.ds(pl.multiple_of(t * share, share), share)
    chosen_v[own_cells, :] = cells_sum.astype(BF16)
    chosen_copies = []
    for d in range(1, tp):
        copy = to_tp(
            chosen_v.at[own_cells, :],
            chosen_v.at[own_cells, :],
            chosen_s.at[d],
            chosen_r.at[d],
            lax.rem(t + d, tp),
        )
        copy.start()
        chosen_copies.append(copy)

    cell = lax.broadcasted_iota(jnp.int32, (1, MERGED), 1)
    row_cell, col_cell = cell // 8, cell % 8
    g0, g1 = about[0:1, :MERGED], about[1:2, :MERGED]
    usable = (row_cell < g0) & (col_cell < g1) & (present[:, :MERGED] > 0)
    target = jnp.where(usable, about[3:4, :MERGED] + row_cell * g1 + col_cell, -1)
    table = (
        lax.broadcasted_iota(jnp.int32, (rows, MERGED), 0) == target
    ).astype(F32)
    covered = jnp.max(table, axis=1, keepdims=True)
    for copy in chosen_copies:
        copy.wait_recv()
    placed = matmul(table.astype(BF16), chosen_v[...])
    prompt_in = jnp.where(covered > 0, placed, token_rows)

    normed = normalize(prompt_in)
    load_tqkv.wait()
    key_v[0:rows, :] = matmul_rows(normed, tqkv_v[1]).astype(BF16)
    for hop in range(1, hops + 1):

        @pl.when(me + hop < seq_count)
        def _():
            to_seq(
                key_v.at[pl.ds(0, rows), :],
                key_v.at[pl.ds(hop * rows, rows), :],
                key_s.at[hop],
                key_r.at[hop],
                lax.rem(me + hop, seq_count),
            ).start()

    value_v[0:rows, :] = matmul_rows(normed, tqkv_v[2]).astype(BF16)
    for hop in range(1, hops + 1):

        @pl.when(me + hop < seq_count)
        def _():
            to_seq(
                value_v.at[pl.ds(0, rows), :],
                value_v.at[pl.ds(hop * rows, rows), :],
                value_s.at[hop],
                value_r.at[hop],
                lax.rem(me + hop, seq_count),
            ).start()

        @pl.when(me < hop)
        def _():
            key_v[hop * rows : (hop + 1) * rows, :] = jnp.zeros((rows, width), BF16)
            value_v[hop * rows : (hop + 1) * rows, :] = jnp.zeros((rows, width), BF16)

    query = matmul_rows(normed, tqkv_v[0]).astype(BF16)
    total_keys = key_v.shape[0]
    lane = lax.broadcasted_iota(jnp.int32, (1, total_keys), 1)
    key_position = (me - lane // rows) * rows + lane % rows
    visible = (key_position <= position) & (key_position >= start)
    for hop in range(1, hops + 1):

        @pl.when(me >= hop)
        def _():
            for buffer, send, recv in ((key_v, key_s, key_r), (value_v, value_s, value_r)):
                to_seq(
                    buffer.at[pl.ds(0, rows), :],
                    buffer.at[pl.ds(hop * rows, rows), :],
                    send.at[hop],
                    recv.at[hop],
                    lax.rem(me + hop, seq_count),
                ).wait_recv()

    for index, piece in enumerate(attention(query, key_v[...], value_v[...], visible)):
        text_context[:, index * 128 : index * 128 + piece.shape[1]] = piece

    for copy in term_copies:
        copy.wait_send()
    load_tout.wait()
    quarter = rows // tp
    last_copies = []
    for d in (2, 3, 1):
        peer = lax.rem(t + d, tp)
        last_send[d] = matmul(
            text_context[pl.ds(pl.multiple_of(peer * quarter, quarter), quarter), :], tout_v[...]
        ).astype(BF16)
        copy = to_tp(last_send.at[d], last_got.at[d], last_s.at[d], last_r.at[d], peer)
        copy.start()
        last_copies.append(copy)
    own_rows = pl.ds(pl.multiple_of(t * quarter, quarter), quarter)
    summed = matmul(text_context[own_rows, :], tout_v[...])
    term_v[0:quarter, :] = jnp.zeros((quarter, tout.shape[1]), F32)
    for index in range(tp):

        @pl.when(t == index)
        def _():
            term_v[0:quarter, :] = prompt_in[index * quarter : (index + 1) * quarter, :]

    summed = summed + term_v[0:quarter, :]
    for copy, d in zip(last_copies, (2, 3, 1)):
        copy.wait_recv()
        summed = summed + last_got[d].astype(F32)
    out[own_rows, :] = summed.astype(BF16)
    out_copies = []
    for d in range(1, tp):
        copy = to_tp(
            out.at[own_rows, :], out.at[own_rows, :], out_s.at[d], out_r.at[d], lax.rem(t + d, tp)
        )
        copy.start()
        out_copies.append(copy)
    for copy in tok_copies + half_copies + [cross] + chosen_copies + last_copies:
        copy.wait_send()
    for hop in range(1, hops + 1):

        @pl.when(me + hop < seq_count)
        def _():
            for buffer, send, recv in ((key_v, key_s, key_r), (value_v, value_s, value_r)):
                to_seq(
                    buffer.at[pl.ds(0, rows), :],
                    buffer.at[pl.ds(hop * rows, rows), :],
                    send.at[hop],
                    recv.at[hop],
                    lax.rem(me + hop, seq_count),
                ).wait_send()

    for copy in out_copies:
        copy.wait()


def local(
    seq_count,
    patches,
    picture_grid,
    vision_qkv,
    vision_out,
    merge_weight,
    picture_block,
    picture_offset,
    tokens,
    prompt_lengths,
    text_qkv,
    text_out,
):
    hops = (seq_count + 3) // 4
    count, model = patches.shape[1:]
    rows, width = tokens.shape
    share, quarter = MERGED // 4, rows // 4
    dma = pltpu.SemaphoreType.DMA
    anywhere = pl.BlockSpec(memory_space=pl.ANY)
    scalars = pl.BlockSpec(memory_space=pltpu.SMEM)
    vmem = pl.BlockSpec(memory_space=pltpu.VMEM)
    keys = (hops + 1) * rows
    return pl.pallas_call(
        functools.partial(kernel, seq_count, hops),
        out_shape=jax.ShapeDtypeStruct((rows, model), BF16),
        in_specs=[
            anywhere,
            scalars,
            anywhere,
            anywhere,
            anywhere,
            scalars,
            scalars,
            vmem,
            scalars,
            anywhere,
            anywhere,
        ],
        out_specs=vmem,
        scratch_shapes=[
            pltpu.VMEM((count, model), BF16),
            pltpu.VMEM((3, width, model), BF16),
            pltpu.VMEM((width, model), BF16),
            pltpu.VMEM((model, model), BF16),
            pltpu.VMEM((3, width, model), BF16),
            pltpu.VMEM((width, model), BF16),
            pltpu.VMEM((4, rows, width), BF16),
            pltpu.VMEM((seq_count, 8, 128), jnp.int32),
            pltpu.VMEM((count, width), BF16),
            pltpu.VMEM((2, MERGED, model), BF16),
            pltpu.VMEM((2, MERGED, model), BF16),
            pltpu.VMEM((MERGED, model), BF16),
            pltpu.VMEM((MERGED, model), BF16),
            pltpu.VMEM((MERGED, model), F32),
            pltpu.VMEM((4, share, model), BF16),
            pltpu.VMEM((seq_count, share, model), BF16),
            pltpu.VMEM((MERGED, model), BF16),
            pltpu.VMEM((keys, width), BF16),
            pltpu.VMEM((keys, width), BF16),
            pltpu.VMEM((rows, width), BF16),
            pltpu.VMEM((4, quarter, model), BF16),
            pltpu.VMEM((4, quarter, model), BF16),
            dma((6,)),
            dma((4,)),
            dma((4,)),
            dma((seq_count,)),
            dma((seq_count,)),
            dma((2,)),
            dma((2,)),
            dma((1,)),
            dma((1,)),
            dma((4,)),
            dma((4,)),
            dma((seq_count,)),
            dma((seq_count,)),
            dma((4,)),
            dma((4,)),
            dma((hops + 1,)),
            dma((hops + 1,)),
            dma((hops + 1,)),
            dma((hops + 1,)),
            dma((4,)),
            dma((4,)),
            dma((4,)),
            dma((4,)),
        ],
        compiler_params=pltpu.CompilerParams(
            collective_id=0, has_side_effects=True, vmem_limit_bytes=56 * 1024 * 1024
        ),
    )(
        patches,
        picture_grid,
        jnp.transpose(vision_qkv, (1, 2, 0)),
        vision_out,
        merge_weight,
        picture_block,
        picture_offset,
        tokens,
        prompt_lengths,
        jnp.transpose(text_qkv, (1, 2, 0)),
        text_out,
    )


def solution(mesh):
    placed = (
        P("seq", None, None),
        P("seq", None),
        P(None, None, "tp"),
        P("tp", None),
        P("tp", None, None),
        P("seq"),
        P("seq"),
        P("seq", "tp"),
        P(),
        P(None, None, "tp"),
        P("tp", None),
    )
    return jax.shard_map(
        functools.partial(local, mesh.shape["seq"]),
        mesh=mesh,
        in_specs=placed,
        out_specs=P("seq", None),
        check_vma=False,
    )
```

time: 184 us -> 62.6 us (0.34)
  the two profiles are of different devices: /device:TPU:0 before, /device:TPU:21 now
where the time goes in v1:
time: 62.6 us; the launch traced here: 62.4 us
  Pallas kernels  57.7 us (92%)
  local copies, waits for them, and re-layouts  3.38 us (5%)
  between operations  1.31 us (2%)
    pallas_call x1, Pallas kernels, local(): pl.pallas_call(functools.partial(kernel, seq_count, hops), out_shape=jax....  57.7 us
    unnamed x2, local copies, waits for them, and re-layouts  3.38 us

profile of v1, /device:TPU:21, one launch (start us, length us, event | category | flops | bytes accessed | tf_op | source)
XLA Modules:
  0.0 62.4 jit_solution(17843291100747914495)
XLA Ops:
  1.3 1.6 %copy.12.tokens = bf16[128,352]{1,0:T(8,128)(2,1)} copy(bf16[128,352]{0,1:T(8,128)(2,1)} %param.18) | data formatting | bytes 180224 | tf_op args[7]
  2.9 57.7 %shard_map.109 = bf16[128,1408]{1,0:T(8,128)(2,1)} custom-call(bf16[1,256,1408]{2,1,0:T(8,128)(2,1)} %patches.1, s32[1,2]{1,0:T(1,128)} %grid.1, bf16[3,352,1408]{2,1,0:T(8,128)(2,1)} %bitcast.2, bf16[352,1408]{1,0:T(8,128)(2,1)} %vout.1, bf16[1,1408,1408]{2,1,0:T(8,128)(2,1)} %merge.1, s32[1]{0:T(128)S(6)} %copy.14.block, s32[1]{0:T(128)S(6)} %copy.15.offset, ...), custom_call_target="tpu_custom_call" | custom-call | tf_op jit(solution)/shard_map/pallas_call | solution.py:490
  60.6 1.7 %copy.16 = bf16[128,1408]{1,0:T(8,128)(2,1)} copy(bf16[128,1408]{1,0:T(8,128)(2,1)} %shard_map.109) | data formatting | bytes 720896

commit v2 on v1

v2 whole, which is shorter than its diff:
```python
import functools

import jax
import jax.numpy as jnp
from jax import lax
from jax.experimental import pallas as pl
from jax.experimental.pallas import tpu as pltpu
from jax.sharding import PartitionSpec as P

HEAD = 88
MAXGRID = 16
MERGED = 64
EPSILON = 1e-06
MASKED = -1e30
F32 = jnp.float32
BF16 = jnp.bfloat16


def normalize(values):
    values = values.astype(F32)
    centre = jnp.mean(values, axis=-1, keepdims=True)
    shifted = values - centre
    spread = jnp.mean(shifted * shifted, axis=-1, keepdims=True)
    return (shifted * lax.rsqrt(spread + EPSILON)).astype(BF16)


def matmul(a, b):
    return jnp.dot(a, b, preferred_element_type=F32)


def matmul_rows(a, b):
    return lax.dot_general(a, b, (((1,), (1,)), ((), ())), preferred_element_type=F32)


def attention(query, keys, values, allowed):
    width = query.shape[1]
    parts = [None] * (-(-width // 128))
    for head in range(width // HEAD):
        first, last = head * HEAD, (head + 1) * HEAD
        low, high = first // 128 * 128, min(width, -(-last // 128) * 128)
        lane = lax.broadcasted_iota(jnp.int32, (1, high - low), 1) + low
        inside = (lane >= first) & (lane < last)
        own_query = jnp.where(inside, query[:, low:high].astype(F32), 0.0).astype(BF16)
        own_values = jnp.where(inside, values[:, low:high].astype(F32), 0.0).astype(BF16)
        scores = matmul_rows(own_query, keys[:, low:high])
        scores = jnp.where(allowed, scores * HEAD ** (-0.5), MASKED)
        expons = jnp.exp(scores - jnp.max(scores, axis=-1, keepdims=True))
        total = jnp.sum(expons, axis=-1, keepdims=True)
        context = matmul(expons.astype(BF16), own_values) / total
        for at in range(low, high, 128):
            piece = context[:, at - low : min(high, at + 128) - low]
            slot = at // 128
            parts[slot] = piece if parts[slot] is None else parts[slot] + piece
    return [part.astype(BF16) for part in parts]


def each(count, body):
    if count <= 4:
        for index in range(count):
            body(index)
    else:

        def step(index, _):
            body(index)
            return 0

        lax.fori_loop(0, count, step, 0)


def kernel(
    seq_count,
    hops,
    patches,
    grid,
    vqkv,
    vout,
    merge,
    block,
    offset,
    tokens,
    lengths,
    tqkv,
    tout,
    out,
    patch_v,
    vqkv_v,
    vout_v,
    merge_v,
    tqkv_v,
    tout_v,
    tok_v,
    meta_v,
    context_v,
    context_got,
    cross_send,
    cross_got,
    term_v,
    term_send,
    term_got,
    gathered,
    chosen_v,
    normed_v,
    prompt_v,
    query_v,
    key_v,
    value_v,
    text_context,
    text_got,
    last_send,
    last_got,
    load_sem,
    weight_s,
    weight_r,
    tok_across_s,
    tok_across_r,
    tok_seq_s,
    tok_seq_r,
    tok_side_s,
    tok_side_r,
    meta_s,
    meta_r,
    half_s,
    half_r,
    cross_s,
    cross_r,
    term_s,
    term_r,
    gather_s,
    gather_r,
    relay_s,
    relay_r,
    chosen_s,
    chosen_r,
    last_s,
    last_r,
):
    me = lax.axis_index("seq")
    t = lax.axis_index("tp")
    tp = 4
    rows = tokens.shape[1]
    blocks = hops + 1
    sibling = t + 1 - 2 * lax.rem(t, 2)
    across = lax.rem(t + 2, 4)
    opposite = 3 - t
    partner = me + 1 - 2 * lax.rem(me, 2)

    def load(source, target, index):
        copy = pltpu.make_async_copy(source, target, load_sem.at[index])
        copy.start()
        return copy

    def remote(source, target, send, recv, device):
        return pltpu.make_async_remote_copy(
            src_ref=source,
            dst_ref=target,
            send_sem=send,
            recv_sem=recv,
            device_id=device,
            device_id_type=pl.DeviceIdType.MESH,
        )

    def to_tp(source, target, send, recv, peer):
        return remote(source, target, send, recv, (me, peer))

    def to_seq(source, target, send, recv, peer):
        return remote(source, target, send, recv, (peer, t))

    load_patches = load(patches.at[0], patch_v, 0)
    load_vqkv = load(vqkv, vqkv_v, 1)

    barrier = pltpu.get_barrier_semaphore()
    for d in range(1, tp):
        pl.semaphore_signal(
            barrier, inc=1, device_id=(me, lax.rem(t + d, tp)), device_id_type=pl.DeviceIdType.MESH
        )

    def greet(d, _):
        pl.semaphore_signal(
            barrier,
            inc=1,
            device_id=(lax.rem(me + d, seq_count), t),
            device_id_type=pl.DeviceIdType.MESH,
        )
        return 0

    lax.fori_loop(1, seq_count, greet, 0)

    half_rows, half_cols = grid[0, 0], grid[0, 1]
    count = patch_v.shape[0]
    slot = lax.broadcasted_iota(jnp.int32, (count, count), 0)
    cell = slot % MERGED
    part = slot // MERGED
    source = (2 * (cell // 8) + part // 2) * MAXGRID + 2 * (cell % 8) + part % 2
    order = (source == lax.broadcasted_iota(jnp.int32, (count, count), 1)).astype(F32).astype(BF16)
    load_patches.wait()
    picture = matmul(order, patch_v[...]).astype(BF16)
    patch_v[...] = picture
    normed = normalize(picture)
    key_slot = lax.broadcasted_iota(jnp.int32, (1, count), 1)
    key_cell = key_slot % MERGED
    key_allowed = (key_cell // 8 < half_rows) & (key_cell % 8 < half_cols)
    load_vqkv.wait()
    load_tokens = load(tokens, tok_v.at[0, t], 6)
    load_vout = load(vout, vout_v.at[0], 2)
    load_merge = load(merge.at[0], merge_v, 3)
    load_tqkv = load(tqkv, tqkv_v, 4)
    load_tout = load(tout, tout_v.at[0], 5)
    query = matmul_rows(normed, vqkv_v[0]).astype(BF16)
    keys = matmul_rows(normed, vqkv_v[1]).astype(BF16)
    values = matmul_rows(normed, vqkv_v[2]).astype(BF16)

    field = lax.broadcasted_iota(jnp.int32, (8, 128), 0)
    meta_v[me] = jnp.where(
        field == 0,
        half_rows,
        jnp.where(field == 1, half_cols, jnp.where(field == 2, block[0], offset[0])),
    )
    pl.semaphore_wait(barrier, tp - 1 + seq_count - 1)
    vout_copy = to_tp(vout, vout_v.at[1], weight_s.at[0], weight_r.at[0], sibling)
    vout_copy.start()
    tok_across = to_tp(tokens, tok_v.at[0, t], tok_across_s.at[0], tok_across_r.at[0], across)
    tok_across.start()

    def meta_copy(d):
        return to_seq(
            meta_v.at[me], meta_v.at[me], meta_s.at[d], meta_r.at[d], lax.rem(me + d, seq_count)
        )

    def send_meta(d, _):
        meta_copy(d).start()
        return 0

    lax.fori_loop(1, seq_count, send_meta, 0)

    for index, piece in enumerate(attention(query, keys, values, key_allowed)):
        context_v[:, index * 128 : index * 128 + piece.shape[1]] = piece

    def patch_rows(which):
        return pl.ds(pl.multiple_of(which * MERGED, MERGED), MERGED)

    half_copies = []
    for index, which in ((1, opposite), (0, sibling)):
        copy = to_tp(
            context_v.at[patch_rows(which), :],
            context_got.at[index],
            half_s.at[index],
            half_r.at[index],
            sibling,
        )
        copy.start()
        half_copies.append(copy)
    load_vout.wait()
    far = matmul(context_v[patch_rows(across), :], vout_v[0])
    vout_copy.wait_recv()
    half_copies[0].wait_recv()
    cross_send[...] = (far + matmul(context_got[1], vout_v[1])).astype(BF16)
    cross = to_tp(cross_send, cross_got, cross_s.at[0], cross_r.at[0], across)
    cross.start()
    near = matmul(context_v[patch_rows(t), :], vout_v[0])
    half_copies[1].wait_recv()
    near = near + matmul(context_got[0], vout_v[1])
    hidden = patch_v[patch_rows(t), :].astype(F32) + near

    tout_copy = to_tp(tout, tout_v.at[1], weight_s.at[1], weight_r.at[1], sibling)
    tout_copy.start()
    load_tokens.wait()
    tok_across.wait_recv()

    def tok_seq_copy(hop, index):
        piece = t if index == 0 else across
        return to_seq(
            tok_v.at[0, piece],
            tok_v.at[hop, piece],
            tok_seq_s.at[hop, index],
            tok_seq_r.at[hop, index],
            lax.rem(me + hop, seq_count),
        )

    def tok_side_copy(hop, index):
        piece = t if index == 0 else across
        return to_tp(
            tok_v.at[hop, piece],
            tok_v.at[hop, piece],
            tok_side_s.at[hop, index],
            tok_side_r.at[hop, index],
            sibling,
        )

    def send_tokens(hop):
        for index in range(2):
            tok_seq_copy(hop + 1, index).start()

    each(hops, send_tokens)
    for index in range(2):
        tok_side_copy(0, index).start()

    load_merge.wait()
    cross.wait_recv()
    merged_in = normalize(hidden + cross_got[...].astype(F32))

    share = MERGED // tp
    term_v[...] = matmul(merged_in, merge_v[...])
    term_copies = []
    for d in (2, 3, 1):
        peer = lax.rem(t + d, tp)
        term_send[d] = term_v[pl.ds(pl.multiple_of(peer * share, share), share), :].astype(BF16)
        copy = to_tp(term_send.at[d], term_got.at[d], term_s.at[d], term_r.at[d], peer)
        copy.start()
        term_copies.append(copy)

    def side_tokens(hop):
        for index in range(2):
            tok_seq_copy(hop + 1, index).wait()
            tok_side_copy(hop + 1, index).start()

    each(hops, side_tokens)
    merged = term_v[pl.ds(pl.multiple_of(t * share, share), share), :]
    for copy, d in zip(term_copies, (2, 3, 1)):
        copy.wait_recv()
        merged = merged + term_got[d].astype(F32)
    gathered[me] = merged.astype(BF16)

    def gather_copy(d):
        return to_seq(
            gathered.at[me],
            gathered.at[me],
            gather_s.at[d],
            gather_r.at[d],
            lax.rem(me + 2 * d, seq_count),
        )

    def relay_copy(d):
        piece = lax.rem(me + seq_count - 2 * d, seq_count)
        return to_seq(
            gathered.at[piece], gathered.at[piece], relay_s.at[d], relay_r.at[d], partner
        )

    def send_merged(d):
        gather_copy(d + 1).start()

    each(seq_count // 2 - 1, send_merged)
    relay_copy(0).start()

    def tokens_in(hop):
        for index in range(2):
            tok_side_copy(hop, index).wait()

    each(blocks, tokens_in)
    same = (
        lax.broadcasted_iota(jnp.int32, (rows, rows), 0)
        == lax.broadcasted_iota(jnp.int32, (rows, rows), 1)
    )
    same = same.astype(F32).astype(BF16)

    def block_rows(hop):
        return pl.ds(pl.multiple_of(hop * rows, rows), rows)

    def norm_tokens(hop):
        whole_rows = matmul_rows(same, tok_v[hop].reshape(-1, rows))
        normed_v[block_rows(hop), :] = normalize(whole_rows)

    each(blocks, norm_tokens)
    prompt_v[...] = matmul_rows(same, tok_v[0].reshape(-1, rows)).astype(BF16)

    def relay(d):
        gather_copy(d + 1).wait_recv()
        relay_copy(d + 1).start()

    load_tqkv.wait()
    group = 3 if blocks % 3 == 0 else 1

    def project_keys(index):
        some = pl.ds(pl.multiple_of(index * group * rows, rows), group * rows)
        key_v[some, :] = matmul_rows(normed_v[some, :], tqkv_v[1]).astype(BF16)

    def project_values(index):
        some = pl.ds(pl.multiple_of(index * group * rows, rows), group * rows)
        value_v[some, :] = matmul_rows(normed_v[some, :], tqkv_v[2]).astype(BF16)

    each(blocks // group, project_keys)
    each(seq_count // 2 - 1, relay)
    each(blocks // group, project_values)
    query_v[...] = matmul_rows(normed_v[0:rows, :], tqkv_v[0]).astype(BF16)
    position = lax.broadcasted_iota(jnp.int32, (rows, 1), 0) + me * rows
    start = jnp.zeros((rows, 1), jnp.int32)
    end = jnp.int32(0)
    for index in range(lengths.shape[0]):
        end = end + lengths[index]
        start = jnp.where(end <= position, end, start)

    def meta_arrived(d, _):
        meta_copy(d).wait()
        return 0

    lax.fori_loop(1, seq_count, meta_arrived, 0)

    def relayed(d):
        relay_copy(d).wait_recv()

    each(seq_count // 2, relayed)

    def choose(hop):
        def add(index, cells_sum):
            hit = (meta_v[index][2:3, 0:1] == me - hop).astype(F32)
            return cells_sum + gathered[index].astype(F32) * hit

        cells_sum = jnp.zeros((share, patch_v.shape[1]), F32)
        if seq_count <= 8:
            for index in range(seq_count):
                cells_sum = add(index, cells_sum)
        else:
            cells_sum = lax.fori_loop(0, seq_count, add, cells_sum)
        chosen_v[t, pl.ds(pl.multiple_of(hop * share, share), share), :] = cells_sum.astype(BF16)

    each(blocks, choose)

    def chosen_copy(index, piece, peer):
        return to_tp(
            chosen_v.at[piece], chosen_v.at[piece], chosen_s.at[index], chosen_r.at[index], peer
        )

    chosen_copies = [chosen_copy(0, t, across), chosen_copy(1, t, sibling)]
    for copy in chosen_copies:
        copy.start()

    all_cells = blocks * MERGED
    lane = lax.broadcasted_iota(jnp.int32, (1, all_cells), 1)
    lane_hop = lane % (blocks * share) // share
    lane_cell = lane // (blocks * share) * share + lane % share
    row_cell, col_cell = lane_cell // 8, lane_cell % 8

    def placement(hop):
        def add(index, state):
            about, present = state
            hit = (meta_v[index][2:3, :] == me - hop).astype(jnp.int32)
            return about + meta_v[index] * hit, present + hit

        about, present = lax.fori_loop(
            0, seq_count, add, (jnp.zeros((8, 128), jnp.int32), jnp.zeros((1, 128), jnp.int32))
        )
        g0, g1 = about[0:1, 0:1], about[1:2, 0:1]
        usable = (row_cell < g0) & (col_cell < g1) & (present[:, 0:1] > 0) & (lane_hop == hop)
        target = jnp.where(usable, about[3:4, 0:1] + row_cell * g1 + col_cell, -1)
        table = (lax.broadcasted_iota(jnp.int32, (rows, all_cells), 0) == target).astype(F32)
        return table.astype(BF16), jnp.max(table, axis=1, keepdims=True)

    if blocks <= 4:
        placements = [placement(hop) for hop in range(blocks)]

    def placement_of(hop):
        return placements[hop] if blocks <= 4 else placement(hop)

    chosen_copies[0].wait_recv()
    chosen_copies.append(chosen_copy(2, across, sibling))
    chosen_copies[2].start()
    chosen_copies[1].wait_recv()
    chosen_copies[2].wait_recv()
    cells = chosen_v[...].reshape(all_cells, -1)
    normed = normalize(cells)
    query_cells = matmul_rows(normed, tqkv_v[0]).astype(BF16)
    key_cells = matmul_rows(normed, tqkv_v[1]).astype(BF16)
    value_cells = matmul_rows(normed, tqkv_v[2]).astype(BF16)

    def put(table, covered, cells_here, before):
        return jnp.where(
            covered > 0, matmul(table, cells_here), before.astype(F32)
        ).astype(BF16)

    def put_block(hop):
        table, covered = placement_of(hop)
        here = block_rows(hop)
        key_v[here, :] = put(table, covered, key_cells, key_v[here, :])
        value_v[here, :] = put(table, covered, value_cells, value_v[here, :])

    each(blocks, put_block)
    table, covered = placement_of(0)
    query = put(table, covered, query_cells, query_v[...])

    lane = lax.broadcasted_iota(jnp.int32, (1, blocks * rows), 1)
    key_position = (me - lane // rows) * rows + lane % rows
    visible = (key_position <= position) & (key_position >= start)
    for index, piece in enumerate(attention(query, key_v[...], value_v[...], visible)):
        text_context[:, index * 128 : index * 128 + piece.shape[1]] = piece

    half = rows // 2
    core = lax.rem(t, 2)
    own_half = pl.ds(pl.multiple_of(core * half, half), half)
    side_half = pl.ds(pl.multiple_of((1 - core) * half, half), half)
    side = to_tp(text_context.at[side_half, :], text_got, last_s.at[0], last_r.at[0], sibling)
    side.start()
    load_tout.wait()
    summed = matmul(text_context[own_half, :], tout_v[0])
    tout_copy.wait_recv()
    side.wait_recv()
    summed = (summed + matmul(text_got[...], tout_v[1])).astype(BF16)
    last_send[...] = summed
    last = to_tp(last_send, last_got, last_s.at[1], last_r.at[1], across)
    last.start()
    prompt_v[...] = put(table, covered, cells, prompt_v[...])
    residual = prompt_v[own_half, :].astype(F32)
    last.wait_recv()
    total = summed.astype(F32) + last_got[...].astype(F32)
    out[own_half, :] = (residual + total).astype(BF16)
    done = to_tp(
        out.at[own_half, :], out.at[own_half, :], last_s.at[2], last_r.at[2], sibling
    )
    done.start()

    def sent(d):
        gather_copy(d + 1).wait_send()

    each(seq_count // 2 - 1, sent)

    def handed_on(d):
        relay_copy(d).wait_send()

    each(seq_count // 2, handed_on)
    for copy in [vout_copy, tout_copy, tok_across, cross, side, last]:
        copy.wait_send()
    for copy in half_copies + term_copies + chosen_copies:
        copy.wait_send()
    done.wait()


def local(
    seq_count,
    patches,
    picture_grid,
    vision_qkv,
    vision_out,
    merge_weight,
    picture_block,
    picture_offset,
    tokens,
    prompt_lengths,
    text_qkv,
    text_out,
):
    hops = (seq_count + 3) // 4
    blocks = hops + 1
    count, model = patches.shape[1:]
    rows, width = tokens.shape
    share, half = MERGED // 4, rows // 2
    dma = pltpu.SemaphoreType.DMA
    hbm = pl.BlockSpec(memory_space=pltpu.HBM)
    scalars = pl.BlockSpec(memory_space=pltpu.SMEM)
    vmem = pl.BlockSpec(memory_space=pltpu.VMEM)
    return pl.pallas_call(
        functools.partial(kernel, seq_count, hops),
        out_shape=jax.ShapeDtypeStruct((rows, model), BF16),
        in_specs=[hbm, scalars, hbm, hbm, hbm, scalars, scalars, hbm, scalars, hbm, hbm],
        out_specs=vmem,
        scratch_shapes=[
            pltpu.VMEM((count, model), BF16),
            pltpu.VMEM((3, width, model), BF16),
            pltpu.VMEM((2, width, model), BF16),
            pltpu.VMEM((model, model), BF16),
            pltpu.VMEM((3, width, model), BF16),
            pltpu.VMEM((2, width, model), BF16),
            pltpu.VMEM((blocks, 4, width, rows), BF16),
            pltpu.VMEM((seq_count, 8, 128), jnp.int32),
            pltpu.VMEM((count, width), BF16),
            pltpu.VMEM((2, MERGED, width), BF16),
            pltpu.VMEM((MERGED, model), BF16),
            pltpu.VMEM((MERGED, model), BF16),
            pltpu.VMEM((MERGED, model), F32),
            pltpu.VMEM((4, share, model), BF16),
            pltpu.VMEM((4, share, model), BF16),
            pltpu.VMEM((seq_count, share, model), BF16),
            pltpu.VMEM((4, blocks * share, model), BF16),
            pltpu.VMEM((blocks * rows, model), BF16),
            pltpu.VMEM((rows, model), BF16),
            pltpu.VMEM((rows, width), BF16),
            pltpu.VMEM((blocks * rows, width), BF16),
            pltpu.VMEM((blocks * rows, width), BF16),
            pltpu.VMEM((rows, width), BF16),
            pltpu.VMEM((half, width), BF16),
            pltpu.VMEM((half, model), BF16),
            pltpu.VMEM((half, model), BF16),
            dma((7,)),
            dma((2,)),
            dma((2,)),
            dma((1,)),
            dma((1,)),
            dma((blocks, 2)),
            dma((blocks, 2)),
            dma((blocks, 2)),
            dma((blocks, 2)),
            dma((seq_count,)),
            dma((seq_count,)),
            dma((2,)),
            dma((2,)),
            dma((1,)),
            dma((1,)),
            dma((4,)),
            dma((4,)),
            dma((seq_count,)),
            dma((seq_count,)),
            dma((seq_count,)),
            dma((seq_count,)),
            dma((3,)),
            dma((3,)),
            dma((3,)),
            dma((3,)),
        ],
        compiler_params=pltpu.CompilerParams(
            collective_id=0, has_side_effects=True, vmem_limit_bytes=56 * 1024 * 1024
        ),
    )(
        patches,
        picture_grid,
        jnp.transpose(vision_qkv, (1, 2, 0)),
        vision_out,
        merge_weight,
        picture_block,
        picture_offset,
        tokens.T,
        prompt_lengths,
        jnp.transpose(text_qkv, (1, 2, 0)),
        text_out,
    )


def solution(mesh):
    placed = (
        P("seq", None, None),
        P("seq", None),
        P(None, None, "tp"),
        P("tp", None),
        P("tp", None, None),
        P("seq"),
        P("seq"),
        P("seq", "tp"),
        P(),
        P(None, None, "tp"),
        P("tp", None),
    )
    return jax.shard_map(
        functools.partial(local, mesh.shape["seq"]),
        mesh=mesh,
        in_specs=placed,
        out_specs=P("seq", None),
        check_vma=False,
    )
```

time: 62.6 us -> 50.5 us (0.81)
  the two profiles are of different devices: /device:TPU:21 before, /device:TPU:0 now
where the time goes in v2:
time: 50.5 us; the launch traced here: 50.4 us
  Pallas kernels  47.3 us (94%)
  local copies, waits for them, and re-layouts  1.75 us (3%)
  between operations  1.3 us (3%)
    pallas_call x1, Pallas kernels, local(): pl.pallas_call(functools.partial(kernel, seq_count, hops), out_shape=jax....  47.3 us
    unnamed x1, local copies, waits for them, and re-layouts  1.75 us

profile of v2, /device:TPU:0, one launch (start us, length us, event | category | flops | bytes accessed | tf_op | source)
XLA Modules:
  0.0 50.4 jit_solution(5409547761077204691)
XLA Ops:
  1.3 47.3 %shard_map.109 = bf16[128,1408]{1,0:T(8,128)(2,1)} custom-call(bf16[1,256,1408]{2,1,0:T(8,128)(2,1)} %patches.1, s32[1,2]{1,0:T(1,128)} %grid.1, bf16[3,352,1408]{2,1,0:T(8,128)(2,1)} %bitcast.3, bf16[352,1408]{1,0:T(8,128)(2,1)} %vout.1, bf16[1,1408,1408]{2,1,0:T(8,128)(2,1)} %merge.1, s32[1]{0:T(128)S(6)} %copy.13.block, s32[1]{0:T(128)S(6)} %copy.14.offset, ...), custom_call_target="tpu_custom_call" | custom-call | tf_op jit(solution)/shard_map/pallas_call | solution.py:548
  48.6 1.7 %copy.15 = bf16[128,1408]{1,0:T(8,128)(2,1)} copy(bf16[128,1408]{1,0:T(8,128)(2,1)} %shard_map.109) | data formatting | bytes 720896

commit v3 on v2

--- a/solution.py
+++ b/solution.py
@@ -99,6 +99,8 @@
     term_got,
     gathered,
     chosen_v,
+    cells_normed,
+    patch_query,
     normed_v,
     prompt_v,
     query_v,
@@ -205,7 +207,7 @@
     load_merge = load(merge.at[0], merge_v, 3)
     load_tqkv = load(tqkv, tqkv_v, 4)
     load_tout = load(tout, tout_v.at[0], 5)
-    query = matmul_rows(normed, vqkv_v[0]).astype(BF16)
+    patch_query[...] = matmul_rows(normed, vqkv_v[0]).astype(BF16)
     keys = matmul_rows(normed, vqkv_v[1]).astype(BF16)
     values = matmul_rows(normed, vqkv_v[2]).astype(BF16)
 
@@ -232,14 +234,18 @@
 
     lax.fori_loop(1, seq_count, send_meta, 0)
 
-    for index, piece in enumerate(attention(query, keys, values, key_allowed)):
-        context_v[:, index * 128 : index * 128 + piece.shape[1]] = piece
-
     def patch_rows(which):
         return pl.ds(pl.multiple_of(which * MERGED, MERGED), MERGED)
 
-    half_copies = []
-    for index, which in ((1, opposite), (0, sibling)):
+    def attend_patches(first, second):
+        pair = (first, second)
+        asking = jnp.concatenate([patch_query[patch_rows(which), :] for which in pair], axis=0)
+        for index, piece in enumerate(attention(asking, keys, values, key_allowed)):
+            lanes = pl.ds(index * 128, piece.shape[1])
+            for place, which in enumerate(pair):
+                context_v[patch_rows(which), lanes] = piece[place * MERGED : (place + 1) * MERGED]
+
+    def share_context(index, which):
         copy = to_tp(
             context_v.at[patch_rows(which), :],
             context_got.at[index],
@@ -248,7 +254,10 @@
             sibling,
         )
         copy.start()
-        half_copies.append(copy)
+        return copy
+
+    attend_patches(opposite, across)
+    half_copies = [share_context(1, opposite)]
     load_vout.wait()
     far = matmul(context_v[patch_rows(across), :], vout_v[0])
     vout_copy.wait_recv()
@@ -256,11 +265,6 @@
     cross_send[...] = (far + matmul(context_got[1], vout_v[1])).astype(BF16)
     cross = to_tp(cross_send, cross_got, cross_s.at[0], cross_r.at[0], across)
     cross.start()
-    near = matmul(context_v[patch_rows(t), :], vout_v[0])
-    half_copies[1].wait_recv()
-    near = near + matmul(context_got[0], vout_v[1])
-    hidden = patch_v[patch_rows(t), :].astype(F32) + near
-
     tout_copy = to_tp(tout, tout_v.at[1], weight_s.at[1], weight_r.at[1], sibling)
     tout_copy.start()
     load_tokens.wait()
@@ -293,6 +297,13 @@
     each(hops, send_tokens)
     for index in range(2):
         tok_side_copy(0, index).start()
+
+    attend_patches(sibling, t)
+    half_copies.append(share_context(0, sibling))
+    near = matmul(context_v[patch_rows(t), :], vout_v[0])
+    half_copies[1].wait_recv()
+    near = near + matmul(context_got[0], vout_v[1])
+    hidden = patch_v[patch_rows(t), :].astype(F32) + near
 
     load_merge.wait()
     cross.wait_recv()
@@ -313,7 +324,26 @@
             tok_seq_copy(hop + 1, index).wait()
             tok_side_copy(hop + 1, index).start()
 
-    each(hops, side_tokens)
+    def tokens_in(hop):
+        for index in range(2):
+            tok_side_copy(hop, index).wait()
+
+    same = (
+        lax.broadcasted_iota(jnp.int32, (rows, rows), 0)
+        == lax.broadcasted_iota(jnp.int32, (rows, rows), 1)
+    )
+    same = same.astype(F32).astype(BF16)
+
+    def block_rows(hop):
+        return pl.ds(pl.multiple_of(hop * rows, rows), rows)
+
+    def norm_tokens(hop):
+        whole_rows = matmul_rows(same, tok_v[hop].reshape(-1, rows))
+        normed_v[block_rows(hop), :] = normalize(whole_rows)
+        return whole_rows
+
+    tokens_in(0)
+    prompt_v[...] = norm_tokens(0).astype(BF16)
     merged = term_v[pl.ds(pl.multiple_of(t * share, share), share), :]
     for copy, d in zip(term_copies, (2, 3, 1)):
         copy.wait_recv()
@@ -341,52 +371,41 @@
     each(seq_count // 2 - 1, send_merged)
     relay_copy(0).start()
 
-    def tokens_in(hop):
-        for index in range(2):
-            tok_side_copy(hop, index).wait()
-
-    each(blocks, tokens_in)
-    same = (
-        lax.broadcasted_iota(jnp.int32, (rows, rows), 0)
-        == lax.broadcasted_iota(jnp.int32, (rows, rows), 1)
-    )
-    same = same.astype(F32).astype(BF16)
-
-    def block_rows(hop):
-        return pl.ds(pl.multiple_of(hop * rows, rows), rows)
-
-    def norm_tokens(hop):
-        whole_rows = matmul_rows(same, tok_v[hop].reshape(-1, rows))
-        normed_v[block_rows(hop), :] = normalize(whole_rows)
-
-    each(blocks, norm_tokens)
-    prompt_v[...] = matmul_rows(same, tok_v[0].reshape(-1, rows)).astype(BF16)
+    each(hops, side_tokens)
+    load_tqkv.wait()
+    query_v[...] = matmul_rows(normed_v[0:rows, :], tqkv_v[0]).astype(BF16)
 
     def relay(d):
         gather_copy(d + 1).wait_recv()
         relay_copy(d + 1).start()
 
-    load_tqkv.wait()
+    def norm_earlier(hop):
+        tokens_in(hop + 1)
+        norm_tokens(hop + 1)
+
+    each(seq_count // 2 - 1, relay)
+    each(hops, norm_earlier)
     group = 3 if blocks % 3 == 0 else 1
 
-    def project_keys(index):
+    def project(index):
         some = pl.ds(pl.multiple_of(index * group * rows, rows), group * rows)
         key_v[some, :] = matmul_rows(normed_v[some, :], tqkv_v[1]).astype(BF16)
-
-    def project_values(index):
-        some = pl.ds(pl.multiple_of(index * group * rows, rows), group * rows)
         value_v[some, :] = matmul_rows(normed_v[some, :], tqkv_v[2]).astype(BF16)
 
-    each(blocks // group, project_keys)
-    each(seq_count // 2 - 1, relay)
-    each(blocks // group, project_values)
-    query_v[...] = matmul_rows(normed_v[0:rows, :], tqkv_v[0]).astype(BF16)
-    position = lax.broadcasted_iota(jnp.int32, (rows, 1), 0) + me * rows
-    start = jnp.zeros((rows, 1), jnp.int32)
-    end = jnp.int32(0)
-    for index in range(lengths.shape[0]):
-        end = end + lengths[index]
-        start = jnp.where(end <= position, end, start)
+    each(blocks // group, project)
+    half = rows // 2
+    core = lax.rem(t, 2)
+
+    def visible_to(which):
+        position = lax.broadcasted_iota(jnp.int32, (half, 1), 0) + me * rows + which * half
+        start = jnp.zeros((half, 1), jnp.int32)
+        end = jnp.int32(0)
+        for index in range(lengths.shape[0]):
+            end = end + lengths[index]
+            start = jnp.where(end <= position, end, start)
+        lane = lax.broadcasted_iota(jnp.int32, (1, blocks * rows), 1)
+        key_position = (me - lane // rows) * rows + lane % rows
+        return (key_position <= position) & (key_position >= start)
 
     def meta_arrived(d, _):
         meta_copy(d).wait()
@@ -450,13 +469,16 @@
     def placement_of(hop):
         return placements[hop] if blocks <= 4 else placement(hop)
 
+    cells_normed[t] = normalize(chosen_v[t])
+    chosen_copies[1].wait_recv()
+    cells_normed[sibling] = normalize(chosen_v[sibling])
     chosen_copies[0].wait_recv()
     chosen_copies.append(chosen_copy(2, across, sibling))
     chosen_copies[2].start()
-    chosen_copies[1].wait_recv()
+    cells_normed[across] = normalize(chosen_v[across])
     chosen_copies[2].wait_recv()
-    cells = chosen_v[...].reshape(all_cells, -1)
-    normed = normalize(cells)
+    cells_normed[opposite] = normalize(chosen_v[opposite])
+    normed = cells_normed[...].reshape(all_cells, -1)
     query_cells = matmul_rows(normed, tqkv_v[0]).astype(BF16)
     key_cells = matmul_rows(normed, tqkv_v[1]).astype(BF16)
     value_cells = matmul_rows(normed, tqkv_v[2]).astype(BF16)
@@ -474,20 +496,21 @@
 
     each(blocks, put_block)
     table, covered = placement_of(0)
-    query = put(table, covered, query_cells, query_v[...])
-
-    lane = lax.broadcasted_iota(jnp.int32, (1, blocks * rows), 1)
-    key_position = (me - lane // rows) * rows + lane % rows
-    visible = (key_position <= position) & (key_position >= start)
-    for index, piece in enumerate(attention(query, key_v[...], value_v[...], visible)):
-        text_context[:, index * 128 : index * 128 + piece.shape[1]] = piece
-
-    half = rows // 2
-    core = lax.rem(t, 2)
+    query_v[...] = put(table, covered, query_cells, query_v[...])
+
     own_half = pl.ds(pl.multiple_of(core * half, half), half)
     side_half = pl.ds(pl.multiple_of((1 - core) * half, half), half)
+
+    def attend_half(which, here):
+        visible = visible_to(which)
+        pieces = attention(query_v[here, :], key_v[...], value_v[...], visible)
+        for index, piece in enumerate(pieces):
+            text_context[here, pl.ds(index * 128, piece.shape[1])] = piece
+
+    attend_half(1 - core, side_half)
     side = to_tp(text_context.at[side_half, :], text_got, last_s.at[0], last_r.at[0], sibling)
     side.start()
+    attend_half(core, own_half)
     load_tout.wait()
     summed = matmul(text_context[own_half, :], tout_v[0])
     tout_copy.wait_recv()
@@ -496,7 +519,7 @@
     last_send[...] = summed
     last = to_tp(last_send, last_got, last_s.at[1], last_r.at[1], across)
     last.start()
-    prompt_v[...] = put(table, covered, cells, prompt_v[...])
+    prompt_v[...] = put(table, covered, chosen_v[...].reshape(all_cells, -1), prompt_v[...])
     residual = prompt_v[own_half, :].astype(F32)
     last.wait_recv()
     total = summed.astype(F32) + last_got[...].astype(F32)
@@ -547,7 +570,7 @@
     vmem = pl.BlockSpec(memory_space=pltpu.VMEM)
     return pl.pallas_call(
         functools.partial(kernel, seq_count, hops),
-        out_shape=jax.ShapeDtypeStruct((rows, model), BF16),
+        out_shape=pltpu.VMEM((rows, model), BF16),
         in_specs=[hbm, scalars, hbm, hbm, hbm, scalars, scalars, hbm, scalars, hbm, hbm],
         out_specs=vmem,
         scratch_shapes=[
@@ -568,6 +591,8 @@
             pltpu.VMEM((4, share, model), BF16),
             pltpu.VMEM((seq_count, share, model), BF16),
             pltpu.VMEM((4, blocks * share, model), BF16),
+            pltpu.VMEM((4, blocks * share, model), BF16),
+            pltpu.VMEM((count, width), BF16),
             pltpu.VMEM((blocks * rows, model), BF16),
             pltpu.VMEM((rows, model), BF16),
             pltpu.VMEM((rows, width), BF16),

time: 50.5 us -> 49.7 us (0.984)
  local copies, waits for them, and re-layouts: 1.75 us -> 0.74 us
    unnamed x1, local copies, waits for them, and re-layouts: 1.75 us -> 0.74 us
where the time goes in v3:
time: 49.7 us; the launch traced here: 49.5 us
  Pallas kernels  47.5 us (96%)
  between operations  1.3 us (3%)
  local copies, waits for them, and re-layouts  0.74 us (1%)
    pallas_call x1, Pallas kernels, local(): pl.pallas_call(functools.partial(kernel, seq_count, hops), out_shape=pltp...  47.5 us

profile of v3, /device:TPU:0, one launch (start us, length us, event | category | flops | bytes accessed | tf_op | source)
XLA Modules:
  0.0 49.5 jit_solution(5039983838068451477)
XLA Ops:
  1.3 47.5 %shard_map.109 = bf16[128,1408]{1,0:T(8,128)(2,1)S(1)} custom-call(bf16[1,256,1408]{2,1,0:T(8,128)(2,1)} %patches.1, s32[1,2]{1,0:T(1,128)} %grid.1, bf16[3,352,1408]{2,1,0:T(8,128)(2,1)} %bitcast.3, bf16[352,1408]{1,0:T(8,128)(2,1)} %vout.1, bf16[1,1408,1408]{2,1,0:T(8,128)(2,1)} %merge.1, s32[1]{0:T(128)S(6)} %copy.14.block, s32[1]{0:T(128)S(6)} %copy.15.offset, ...), custom_call_target="tpu_custom_call" | custom-call | tf_op jit(solution)/shard_map/pallas_call | solution.py:571
  48.8 0.7 %copy.13 = bf16[128,1408]{1,0:T(8,128)(2,1)} copy(bf16[128,1408]{1,0:T(8,128)(2,1)S(1)} %shard_map.109) | data formatting | bytes 720896

commit v4 on v3

--- a/solution.py
+++ b/solution.py
@@ -11,7 +11,8 @@
 MAXGRID = 16
 MERGED = 64
 EPSILON = 1e-06
-MASKED = -1e30
+MASKED = -1e31
+LOG2E = 1.4426950408889634
 F32 = jnp.float32
 BF16 = jnp.bfloat16
 
@@ -39,14 +40,13 @@
         first, last = head * HEAD, (head + 1) * HEAD
         low, high = first // 128 * 128, min(width, -(-last // 128) * 128)
         lane = lax.broadcasted_iota(jnp.int32, (1, high - low), 1) + low
-        inside = (lane >= first) & (lane < last)
-        own_query = jnp.where(inside, query[:, low:high].astype(F32), 0.0).astype(BF16)
-        own_values = jnp.where(inside, values[:, low:high].astype(F32), 0.0).astype(BF16)
-        scores = matmul_rows(own_query, keys[:, low:high])
-        scores = jnp.where(allowed, scores * HEAD ** (-0.5), MASKED)
-        expons = jnp.exp(scores - jnp.max(scores, axis=-1, keepdims=True))
+        inside = ((lane >= first) & (lane < last)).astype(F32).astype(BF16)
+        scores = matmul_rows(query[:, low:high] * inside, keys[:, low:high])
+        scores = jnp.where(allowed, scores, MASKED)
+        top = jnp.max(scores, axis=-1, keepdims=True)
+        expons = jnp.exp2((scores - top) * (HEAD ** (-0.5) * LOG2E))
         total = jnp.sum(expons, axis=-1, keepdims=True)
-        context = matmul(expons.astype(BF16), own_values) / total
+        context = matmul(expons.astype(BF16), values[:, low:high] * inside) * (1.0 / total)
         for at in range(low, high, 128):
             piece = context[:, at - low : min(high, at + 128) - low]
             slot = at // 128
@@ -189,50 +189,74 @@
 
     half_rows, half_cols = grid[0, 0], grid[0, 1]
     count = patch_v.shape[0]
-    slot = lax.broadcasted_iota(jnp.int32, (count, count), 0)
-    cell = slot % MERGED
-    part = slot // MERGED
-    source = (2 * (cell // 8) + part // 2) * MAXGRID + 2 * (cell % 8) + part % 2
-    order = (source == lax.broadcasted_iota(jnp.int32, (count, count), 1)).astype(F32).astype(BF16)
+
+    def ordering(first, size):
+        slot = lax.broadcasted_iota(jnp.int32, (size, count), 0) + first
+        cell = slot % MERGED
+        part = slot // MERGED
+        source = (2 * (cell // 8) + part // 2) * MAXGRID + 2 * (cell % 8) + part % 2
+        picked = source == lax.broadcasted_iota(jnp.int32, (size, count), 1)
+        return picked.astype(F32).astype(BF16)
+
+    order = ordering(0, count)
+    key_slot = lax.broadcasted_iota(jnp.int32, (1, count), 1)
+    key_allowed = (key_slot // MAXGRID < 2 * half_rows) & (key_slot % MAXGRID < 2 * half_cols)
     load_patches.wait()
-    picture = matmul(order, patch_v[...]).astype(BF16)
-    patch_v[...] = picture
-    normed = normalize(picture)
-    key_slot = lax.broadcasted_iota(jnp.int32, (1, count), 1)
-    key_cell = key_slot % MERGED
-    key_allowed = (key_cell // 8 < half_rows) & (key_cell % 8 < half_cols)
+    normed = normalize(patch_v[...])
+
+    pl.semaphore_wait(barrier, tp - 1 + seq_count - 1)
+    tok_across = to_tp(tokens, tok_v.at[0, t], tok_across_s.at[0], tok_across_r.at[0], across)
+    tok_across.start()
+    load_tokens = load(tokens, tok_v.at[0, t], 6)
+
+    def tok_seq_copy(hop, index):
+        piece = t if index == 0 else across
+        return to_seq(
+            tok_v.at[0, piece],
+            tok_v.at[hop, piece],
+            tok_seq_s.at[hop, index],
+            tok_seq_r.at[hop, index],
+            lax.rem(me + hop, seq_count),
+        )
+
+    def tok_side_copy(hop, index):
+        piece = t if index == 0 else across
+        return to_tp(
+            tok_v.at[hop, piece],
+            tok_v.at[hop, piece],
+            tok_side_s.at[hop, index],
+            tok_side_r.at[hop, index],
+            sibling,
+        )
+
+    def send_own(hop):
+        tok_seq_copy(hop + 1, 0).start()
+
+    def send_across(hop):
+        tok_seq_copy(hop + 1, 1).start()
+
     load_vqkv.wait()
-    load_tokens = load(tokens, tok_v.at[0, t], 6)
     load_vout = load(vout, vout_v.at[0], 2)
     load_merge = load(merge.at[0], merge_v, 3)
+    load_tokens.wait()
+    each(hops, send_own)
+    vout_copy = to_tp(vout, vout_v.at[1], weight_s.at[0], weight_r.at[0], sibling)
+    vout_copy.start()
     load_tqkv = load(tqkv, tqkv_v, 4)
     load_tout = load(tout, tout_v.at[0], 5)
-    patch_query[...] = matmul_rows(normed, vqkv_v[0]).astype(BF16)
+    query = matmul_rows(normed, vqkv_v[0]).astype(BF16)
+    patch_query[...] = matmul(order, query).astype(BF16)
     keys = matmul_rows(normed, vqkv_v[1]).astype(BF16)
     values = matmul_rows(normed, vqkv_v[2]).astype(BF16)
-
-    field = lax.broadcasted_iota(jnp.int32, (8, 128), 0)
-    meta_v[me] = jnp.where(
-        field == 0,
-        half_rows,
-        jnp.where(field == 1, half_cols, jnp.where(field == 2, block[0], offset[0])),
-    )
-    pl.semaphore_wait(barrier, tp - 1 + seq_count - 1)
-    vout_copy = to_tp(vout, vout_v.at[1], weight_s.at[0], weight_r.at[0], sibling)
-    vout_copy.start()
-    tok_across = to_tp(tokens, tok_v.at[0, t], tok_across_s.at[0], tok_across_r.at[0], across)
-    tok_across.start()
+    tok_across.wait_recv()
+    each(hops, send_across)
+    for index in range(2):
+        tok_side_copy(0, index).start()
 
     def meta_copy(d):
         return to_seq(
             meta_v.at[me], meta_v.at[me], meta_s.at[d], meta_r.at[d], lax.rem(me + d, seq_count)
         )
-
-    def send_meta(d, _):
-        meta_copy(d).start()
-        return 0
-
-    lax.fori_loop(1, seq_count, send_meta, 0)
 
     def patch_rows(which):
         return pl.ds(pl.multiple_of(which * MERGED, MERGED), MERGED)
@@ -265,45 +289,48 @@
     cross_send[...] = (far + matmul(context_got[1], vout_v[1])).astype(BF16)
     cross = to_tp(cross_send, cross_got, cross_s.at[0], cross_r.at[0], across)
     cross.start()
-    tout_copy = to_tp(tout, tout_v.at[1], weight_s.at[1], weight_r.at[1], sibling)
-    tout_copy.start()
-    load_tokens.wait()
-    tok_across.wait_recv()
-
-    def tok_seq_copy(hop, index):
-        piece = t if index == 0 else across
-        return to_seq(
-            tok_v.at[0, piece],
-            tok_v.at[hop, piece],
-            tok_seq_s.at[hop, index],
-            tok_seq_r.at[hop, index],
-            lax.rem(me + hop, seq_count),
-        )
-
-    def tok_side_copy(hop, index):
-        piece = t if index == 0 else across
-        return to_tp(
-            tok_v.at[hop, piece],
-            tok_v.at[hop, piece],
-            tok_side_s.at[hop, index],
-            tok_side_r.at[hop, index],
-            sibling,
-        )
-
-    def send_tokens(hop):
-        for index in range(2):
-            tok_seq_copy(hop + 1, index).start()
-
-    each(hops, send_tokens)
-    for index in range(2):
-        tok_side_copy(0, index).start()
-
     attend_patches(sibling, t)
     half_copies.append(share_context(0, sibling))
     near = matmul(context_v[patch_rows(t), :], vout_v[0])
     half_copies[1].wait_recv()
     near = near + matmul(context_got[0], vout_v[1])
-    hidden = patch_v[patch_rows(t), :].astype(F32) + near
+    hidden = matmul(ordering(t * MERGED, MERGED), patch_v[...]) + near
+    tout_copy = to_tp(tout, tout_v.at[1], weight_s.at[1], weight_r.at[1], sibling)
+    tout_copy.start()
+
+    field = lax.broadcasted_iota(jnp.int32, (8, 128), 0)
+    meta_v[me] = jnp.where(
+        field == 0,
+        half_rows,
+        jnp.where(field == 1, half_cols, jnp.where(field == 2, block[0], offset[0])),
+    )
+
+    def send_meta(d, _):
+        meta_copy(d).start()
+        return 0
+
+    lax.fori_loop(1, seq_count, send_meta, 0)
+
+    same = (
+        lax.broadcasted_iota(jnp.int32, (rows, rows), 0)
+        == lax.broadcasted_iota(jnp.int32, (rows, rows), 1)
+    )
+    same = same.astype(F32).astype(BF16)
+
+    def block_rows(hop):
+        return pl.ds(pl.multiple_of(hop * rows, rows), rows)
+
+    def norm_tokens(hop):
+        whole_rows = matmul_rows(same, tok_v[hop].reshape(-1, rows))
+        normed_v[block_rows(hop), :] = normalize(whole_rows)
+        return whole_rows
+
+    def tokens_in(hop):
+        for index in range(2):
+            tok_side_copy(hop, index).wait()
+
+    tokens_in(0)
+    prompt_v[...] = norm_tokens(0).astype(BF16)
 
     load_merge.wait()
     cross.wait_recv()
@@ -324,26 +351,7 @@
             tok_seq_copy(hop + 1, index).wait()
             tok_side_copy(hop + 1, index).start()
 
-    def tokens_in(hop):
-        for index in range(2):
-            tok_side_copy(hop, index).wait()
-
-    same = (
-        lax.broadcasted_iota(jnp.int32, (rows, rows), 0)
-        == lax.broadcasted_iota(jnp.int32, (rows, rows), 1)
-    )
-    same = same.astype(F32).astype(BF16)
-
-    def block_rows(hop):
-        return pl.ds(pl.multiple_of(hop * rows, rows), rows)
-
-    def norm_tokens(hop):
-        whole_rows = matmul_rows(same, tok_v[hop].reshape(-1, rows))
-        normed_v[block_rows(hop), :] = normalize(whole_rows)
-        return whole_rows
-
-    tokens_in(0)
-    prompt_v[...] = norm_tokens(0).astype(BF16)
+    each(hops, side_tokens)
     merged = term_v[pl.ds(pl.multiple_of(t * share, share), share), :]
     for copy, d in zip(term_copies, (2, 3, 1)):
         copy.wait_recv()
@@ -371,7 +379,6 @@
     each(seq_count // 2 - 1, send_merged)
     relay_copy(0).start()
 
-    each(hops, side_tokens)
     load_tqkv.wait()
     query_v[...] = matmul_rows(normed_v[0:rows, :], tqkv_v[0]).astype(BF16)
 

time: 49.7 us -> 51.5 us (1.036)
  Pallas kernels: 47.5 us -> 49.3 us
    pallas_call x1, Pallas kernels: 47.5 us -> 49.3 us  [local(): pl.pallas_call(functools.partial(kernel, seq_count, hops), out_shape=pltp...]
where the time goes in v4:
time: 51.5 us; the launch traced here: 51.3 us
  Pallas kernels  49.3 us (96%)
  between operations  1.3 us (3%)
  local copies, waits for them, and re-layouts  0.74 us (1%)
    pallas_call x1, Pallas kernels, local(): pl.pallas_call(functools.partial(kernel, seq_count, hops), out_shape=pltp...  49.3 us

profile of v4, /device:TPU:0, one launch (start us, length us, event | category | flops | bytes accessed | tf_op | source)
XLA Modules:
  0.0 51.3 jit_solution(12198077359726617077)
XLA Ops:
  1.3 49.3 %shard_map.109 = bf16[128,1408]{1,0:T(8,128)(2,1)S(1)} custom-call(bf16[1,256,1408]{2,1,0:T(8,128)(2,1)} %patches.1, s32[1,2]{1,0:T(1,128)} %grid.1, bf16[3,352,1408]{2,1,0:T(8,128)(2,1)} %bitcast.3, bf16[352,1408]{1,0:T(8,128)(2,1)} %vout.1, bf16[1,1408,1408]{2,1,0:T(8,128)(2,1)} %merge.1, s32[1]{0:T(128)S(6)} %copy.14.block, s32[1]{0:T(128)S(6)} %copy.15.offset, ...), custom_call_target="tpu_custom_call" | custom-call | tf_op jit(solution)/shard_map/pallas_call | solution.py:578
  50.6 0.7 %copy.13 = bf16[128,1408]{1,0:T(8,128)(2,1)} copy(bf16[128,1408]{1,0:T(8,128)(2,1)S(1)} %shard_map.109) | data formatting | bytes 720896

commit v5 on v3

--- a/solution.py
+++ b/solution.py
@@ -11,7 +11,8 @@
 MAXGRID = 16
 MERGED = 64
 EPSILON = 1e-06
-MASKED = -1e30
+MASKED = -1e31
+LOG2E = 1.4426950408889634
 F32 = jnp.float32
 BF16 = jnp.bfloat16
 
@@ -39,14 +40,13 @@
         first, last = head * HEAD, (head + 1) * HEAD
         low, high = first // 128 * 128, min(width, -(-last // 128) * 128)
         lane = lax.broadcasted_iota(jnp.int32, (1, high - low), 1) + low
-        inside = (lane >= first) & (lane < last)
-        own_query = jnp.where(inside, query[:, low:high].astype(F32), 0.0).astype(BF16)
-        own_values = jnp.where(inside, values[:, low:high].astype(F32), 0.0).astype(BF16)
-        scores = matmul_rows(own_query, keys[:, low:high])
-        scores = jnp.where(allowed, scores * HEAD ** (-0.5), MASKED)
-        expons = jnp.exp(scores - jnp.max(scores, axis=-1, keepdims=True))
+        inside = ((lane >= first) & (lane < last)).astype(F32).astype(BF16)
+        scores = matmul_rows(query[:, low:high] * inside, keys[:, low:high])
+        scores = jnp.where(allowed, scores, MASKED)
+        top = jnp.max(scores, axis=-1, keepdims=True)
+        expons = jnp.exp2((scores - top) * (HEAD ** (-0.5) * LOG2E))
         total = jnp.sum(expons, axis=-1, keepdims=True)
-        context = matmul(expons.astype(BF16), own_values) / total
+        context = matmul(expons.astype(BF16), values[:, low:high] * inside) * (1.0 / total)
         for at in range(low, high, 128):
             piece = context[:, at - low : min(high, at + 128) - low]
             slot = at // 128
@@ -189,25 +189,26 @@
 
     half_rows, half_cols = grid[0, 0], grid[0, 1]
     count = patch_v.shape[0]
-    slot = lax.broadcasted_iota(jnp.int32, (count, count), 0)
-    cell = slot % MERGED
-    part = slot // MERGED
-    source = (2 * (cell // 8) + part // 2) * MAXGRID + 2 * (cell % 8) + part % 2
-    order = (source == lax.broadcasted_iota(jnp.int32, (count, count), 1)).astype(F32).astype(BF16)
+
+    def ordering(first, size):
+        slot = lax.broadcasted_iota(jnp.int32, (size, 1), 0) + first
+        row = ((slot >> 3) & 7) * 2 + (slot >> 7)
+        col = (slot & 7) * 2 + ((slot >> 6) & 1)
+        picked = row * MAXGRID + col == lax.broadcasted_iota(jnp.int32, (size, count), 1)
+        return picked.astype(F32).astype(BF16)
+
+    order = ordering(0, count)
+    key_slot = lax.broadcasted_iota(jnp.int32, (1, count), 1)
+    key_allowed = (key_slot >> 4 < 2 * half_rows) & ((key_slot & 15) < 2 * half_cols)
     load_patches.wait()
-    picture = matmul(order, patch_v[...]).astype(BF16)
-    patch_v[...] = picture
-    normed = normalize(picture)
-    key_slot = lax.broadcasted_iota(jnp.int32, (1, count), 1)
-    key_cell = key_slot % MERGED
-    key_allowed = (key_cell // 8 < half_rows) & (key_cell % 8 < half_cols)
+    normed = normalize(patch_v[...])
     load_vqkv.wait()
     load_tokens = load(tokens, tok_v.at[0, t], 6)
     load_vout = load(vout, vout_v.at[0], 2)
     load_merge = load(merge.at[0], merge_v, 3)
     load_tqkv = load(tqkv, tqkv_v, 4)
     load_tout = load(tout, tout_v.at[0], 5)
-    patch_query[...] = matmul_rows(normed, vqkv_v[0]).astype(BF16)
+    patch_query[...] = matmul(order, matmul_rows(normed, vqkv_v[0]).astype(BF16)).astype(BF16)
     keys = matmul_rows(normed, vqkv_v[1]).astype(BF16)
     values = matmul_rows(normed, vqkv_v[2]).astype(BF16)
 
@@ -303,7 +304,7 @@
     near = matmul(context_v[patch_rows(t), :], vout_v[0])
     half_copies[1].wait_recv()
     near = near + matmul(context_got[0], vout_v[1])
-    hidden = patch_v[patch_rows(t), :].astype(F32) + near
+    hidden = matmul(ordering(t * MERGED, MERGED), patch_v[...]) + near
 
     load_merge.wait()
     cross.wait_recv()

time: 49.7 us -> 49.9 us (level)
  no operation moved by 1% of the time
where the time goes in v5:
time: 49.9 us; the launch traced here: 49.7 us
  Pallas kernels  47.7 us (96%)
  between operations  1.3 us (3%)
  local copies, waits for them, and re-layouts  0.74 us (1%)
    pallas_call x1, Pallas kernels, local(): pl.pallas_call(functools.partial(kernel, seq_count, hops), out_shape=pltp...  47.7 us

profile of v5, /device:TPU:0, one launch (start us, length us, event | category | flops | bytes accessed | tf_op | source)
XLA Modules:
  0.0 49.7 jit_solution(8091290509410509703)
XLA Ops:
  1.3 47.7 %shard_map.109 = bf16[128,1408]{1,0:T(8,128)(2,1)S(1)} custom-call(bf16[1,256,1408]{2,1,0:T(8,128)(2,1)} %patches.1, s32[1,2]{1,0:T(1,128)} %grid.1, bf16[3,352,1408]{2,1,0:T(8,128)(2,1)} %bitcast.3, bf16[352,1408]{1,0:T(8,128)(2,1)} %vout.1, bf16[1,1408,1408]{2,1,0:T(8,128)(2,1)} %merge.1, s32[1]{0:T(128)S(6)} %copy.14.block, s32[1]{0:T(128)S(6)} %copy.15.offset, ...), custom_call_target="tpu_custom_call" | custom-call | tf_op jit(solution)/shard_map/pallas_call | solution.py:572
  49.0 0.7 %copy.13 = bf16[128,1408]{1,0:T(8,128)(2,1)} copy(bf16[128,1408]{1,0:T(8,128)(2,1)S(1)} %shard_map.109) | data formatting | bytes 720896

commit v6 on v5

--- a/solution.py
+++ b/solution.py
@@ -91,7 +91,8 @@
     tok_v,
     meta_v,
     context_v,
-    context_got,
+    half_send,
+    half_got,
     cross_send,
     cross_got,
     term_v,
@@ -204,7 +205,7 @@
     normed = normalize(patch_v[...])
     load_vqkv.wait()
     load_tokens = load(tokens, tok_v.at[0, t], 6)
-    load_vout = load(vout, vout_v.at[0], 2)
+    load_vout = load(vout, vout_v, 2)
     load_merge = load(merge.at[0], merge_v, 3)
     load_tqkv = load(tqkv, tqkv_v, 4)
     load_tout = load(tout, tout_v.at[0], 5)
@@ -219,8 +220,6 @@
         jnp.where(field == 1, half_cols, jnp.where(field == 2, block[0], offset[0])),
     )
     pl.semaphore_wait(barrier, tp - 1 + seq_count - 1)
-    vout_copy = to_tp(vout, vout_v.at[1], weight_s.at[0], weight_r.at[0], sibling)
-    vout_copy.start()
     tok_across = to_tp(tokens, tok_v.at[0, t], tok_across_s.at[0], tok_across_r.at[0], across)
     tok_across.start()
 
@@ -246,28 +245,25 @@
             for place, which in enumerate(pair):
                 context_v[patch_rows(which), lanes] = piece[place * MERGED : (place + 1) * MERGED]
 
-    def share_context(index, which):
+    def partial_rows(which):
+        return matmul(context_v[patch_rows(which), :], vout_v[...])
+
+    def share_partial(index, which):
+        half_send[index] = partial_rows(which).astype(BF16)
         copy = to_tp(
-            context_v.at[patch_rows(which), :],
-            context_got.at[index],
-            half_s.at[index],
-            half_r.at[index],
-            sibling,
+            half_send.at[index], half_got.at[index], half_s.at[index], half_r.at[index], sibling
         )
         copy.start()
         return copy
 
     attend_patches(opposite, across)
-    half_copies = [share_context(1, opposite)]
     load_vout.wait()
-    far = matmul(context_v[patch_rows(across), :], vout_v[0])
-    vout_copy.wait_recv()
+    half_copies = [share_partial(1, opposite)]
+    far = partial_rows(across)
     half_copies[0].wait_recv()
-    cross_send[...] = (far + matmul(context_got[1], vout_v[1])).astype(BF16)
+    cross_send[...] = (far + half_got[1].astype(F32)).astype(BF16)
     cross = to_tp(cross_send, cross_got, cross_s.at[0], cross_r.at[0], across)
     cross.start()
-    tout_copy = to_tp(tout, tout_v.at[1], weight_s.at[1], weight_r.at[1], sibling)
-    tout_copy.start()
     load_tokens.wait()
     tok_across.wait_recv()
 
@@ -300,10 +296,10 @@
         tok_side_copy(0, index).start()
 
     attend_patches(sibling, t)
-    half_copies.append(share_context(0, sibling))
-    near = matmul(context_v[patch_rows(t), :], vout_v[0])
+    half_copies.append(share_partial(0, sibling))
+    near = partial_rows(t)
     half_copies[1].wait_recv()
-    near = near + matmul(context_got[0], vout_v[1])
+    near = near + half_got[0].astype(F32)
     hidden = matmul(ordering(t * MERGED, MERGED), patch_v[...]) + near
 
     load_merge.wait()
@@ -371,6 +367,8 @@
 
     each(seq_count // 2 - 1, send_merged)
     relay_copy(0).start()
+    tout_copy = to_tp(tout, tout_v.at[1], weight_s.at[0], weight_r.at[0], sibling)
+    tout_copy.start()
 
     each(hops, side_tokens)
     load_tqkv.wait()
@@ -539,7 +537,7 @@
         relay_copy(d).wait_send()
 
     each(seq_count // 2, handed_on)
-    for copy in [vout_copy, tout_copy, tok_across, cross, side, last]:
+    for copy in [tout_copy, tok_across, cross, side, last]:
         copy.wait_send()
     for copy in half_copies + term_copies + chosen_copies:
         copy.wait_send()
@@ -577,14 +575,15 @@
         scratch_shapes=[
             pltpu.VMEM((count, model), BF16),
             pltpu.VMEM((3, width, model), BF16),
-            pltpu.VMEM((2, width, model), BF16),
+            pltpu.VMEM((width, model), BF16),
             pltpu.VMEM((model, model), BF16),
             pltpu.VMEM((3, width, model), BF16),
             pltpu.VMEM((2, width, model), BF16),
             pltpu.VMEM((blocks, 4, width, rows), BF16),
             pltpu.VMEM((seq_count, 8, 128), jnp.int32),
             pltpu.VMEM((count, width), BF16),
-            pltpu.VMEM((2, MERGED, width), BF16),
+            pltpu.VMEM((2, MERGED, model), BF16),
+            pltpu.VMEM((2, MERGED, model), BF16),
             pltpu.VMEM((MERGED, model), BF16),
             pltpu.VMEM((MERGED, model), BF16),
             pltpu.VMEM((MERGED, model), F32),
@@ -604,8 +603,8 @@
             pltpu.VMEM((half, model), BF16),
             pltpu.VMEM((half, model), BF16),
             dma((7,)),
-            dma((2,)),
-            dma((2,)),
+            dma((1,)),
+            dma((1,)),
             dma((1,)),
             dma((1,)),
             dma((blocks, 2)),

time: 49.9 us -> 49.8 us (level)
  no operation moved by 1% of the time
where the time goes in v6:
time: 49.8 us; the launch traced here: 49.6 us
  Pallas kernels  47.5 us (95%)
  between operations  1.3 us (3%)
  local copies, waits for them, and re-layouts  0.74 us (1%)
    pallas_call x1, Pallas kernels, local(): pl.pallas_call(functools.partial(kernel, seq_count, hops), out_shape=pltp...  47.5 us

profile of v6, /device:TPU:0, one launch (start us, length us, event | category | flops | bytes accessed | tf_op | source)
XLA Modules:
  0.0 49.6 jit_solution(3832077874046620803)
XLA Ops:
  1.3 47.5 %shard_map.109 = bf16[128,1408]{1,0:T(8,128)(2,1)S(1)} custom-call(bf16[1,256,1408]{2,1,0:T(8,128)(2,1)} %patches.1, s32[1,2]{1,0:T(1,128)} %grid.1, bf16[3,352,1408]{2,1,0:T(8,128)(2,1)} %bitcast.3, bf16[352,1408]{1,0:T(8,128)(2,1)} %vout.1, bf16[1,1408,1408]{2,1,0:T(8,128)(2,1)} %merge.1, s32[1]{0:T(128)S(6)} %copy.14.block, s32[1]{0:T(128)S(6)} %copy.15.offset, ...), custom_call_target="tpu_custom_call" | custom-call | tf_op jit(solution)/shard_map/pallas_call | solution.py:570
  48.8 0.7 %copy.13 = bf16[128,1408]{1,0:T(8,128)(2,1)} copy(bf16[128,1408]{1,0:T(8,128)(2,1)S(1)} %shard_map.109) | data formatting | bytes 720896

commit v7 on v3

--- a/solution.py
+++ b/solution.py
@@ -396,9 +396,9 @@
     half = rows // 2
     core = lax.rem(t, 2)
 
-    def visible_to(which):
-        position = lax.broadcasted_iota(jnp.int32, (half, 1), 0) + me * rows + which * half
-        start = jnp.zeros((half, 1), jnp.int32)
+    def visible_keys():
+        position = lax.broadcasted_iota(jnp.int32, (rows, 1), 0) + me * rows
+        start = jnp.zeros((rows, 1), jnp.int32)
         end = jnp.int32(0)
         for index in range(lengths.shape[0]):
             end = end + lengths[index]
@@ -501,16 +501,15 @@
     own_half = pl.ds(pl.multiple_of(core * half, half), half)
     side_half = pl.ds(pl.multiple_of((1 - core) * half, half), half)
 
-    def attend_half(which, here):
-        visible = visible_to(which)
+    def attend_rows(here):
+        visible = visible_keys()
         pieces = attention(query_v[here, :], key_v[...], value_v[...], visible)
         for index, piece in enumerate(pieces):
             text_context[here, pl.ds(index * 128, piece.shape[1])] = piece
 
-    attend_half(1 - core, side_half)
+    attend_rows(pl.ds(0, rows))
     side = to_tp(text_context.at[side_half, :], text_got, last_s.at[0], last_r.at[0], sibling)
     side.start()
-    attend_half(core, own_half)
     load_tout.wait()
     summed = matmul(text_context[own_half, :], tout_v[0])
     tout_copy.wait_recv()

time: 49.7 us -> 48.8 us (0.982)
  Pallas kernels: 47.5 us -> 46.6 us
    pallas_call x1, Pallas kernels: 47.5 us -> 46.6 us  [local(): pl.pallas_call(functools.partial(kernel, seq_count, hops), out_shape=pltp...]
where the time goes in v7:
time: 48.8 us; the launch traced here: 48.7 us
  Pallas kernels  46.6 us (95%)
  between operations  1.3 us (3%)
  local copies, waits for them, and re-layouts  0.74 us (2%)
    pallas_call x1, Pallas kernels, local(): pl.pallas_call(functools.partial(kernel, seq_count, hops), out_shape=pltp...  46.6 us

profile of v7, /device:TPU:0, one launch (start us, length us, event | category | flops | bytes accessed | tf_op | source)
XLA Modules:
  0.0 48.7 jit_solution(12711732028266895931)
XLA Ops:
  1.3 46.6 %shard_map.109 = bf16[128,1408]{1,0:T(8,128)(2,1)S(1)} custom-call(bf16[1,256,1408]{2,1,0:T(8,128)(2,1)} %patches.1, s32[1,2]{1,0:T(1,128)} %grid.1, bf16[3,352,1408]{2,1,0:T(8,128)(2,1)} %bitcast.3, bf16[352,1408]{1,0:T(8,128)(2,1)} %vout.1, bf16[1,1408,1408]{2,1,0:T(8,128)(2,1)} %merge.1, s32[1]{0:T(128)S(6)} %copy.14.block, s32[1]{0:T(128)S(6)} %copy.15.offset, ...), custom_call_target="tpu_custom_call" | custom-call | tf_op jit(solution)/shard_map/pallas_call | solution.py:570
  47.9 0.7 %copy.13 = bf16[128,1408]{1,0:T(8,128)(2,1)} copy(bf16[128,1408]{1,0:T(8,128)(2,1)S(1)} %shard_map.109) | data formatting | bytes 720896
